TPU v7x, 32 devices: a whole 2x2x4 slice. The times are simulated.
32 devices in a mesh: grp: 2 (over x), seq: 16 (over z, y, core).
Axes of the slice: x: 2, y: 2, z: 4, core: 2. Of those that a mesh axis runs over, the one named last changes fastest.
Arguments:
- inputs: bfloat16 [4096, 4096], P(('grp', 'seq')), parts along dimension 0, may hold values from -6 to 6
- in_weight: bfloat16 [4096, 768], replicated, may hold values from -0.09375 to 0.09375
- filter_taps: float32 [2048, 256], P('seq'), may hold values from -6 to 6
- grad_out: bfloat16 [4096, 256], P(('grp', 'seq')), parts along dimension 0, may hold values from -6 to 6
Outputs:
- grad_inputs: bfloat16 [4096, 4096], P(('grp', 'seq')), parts along dimension 0
- grad_weight: float32 [8192, 768], P(('grp', 'seq')), parts along dimension 0
- grad_taps: float32 [4096, 256], P(('grp', 'seq')), parts along dimension 0
There are 2 independent parts, one for each index of `grp`. A program takes and returns all parts, laid end to end along the dimension named above; an argument that names none is the same for every part. Nothing has to cross between parts.
All inputs are finite; a program needn't handle non-finite values.
Results may differ from a plain program's by a relative error of at most 0.0064.
Values sent between devices are 32-bit elements; how exact they have to be, the bound alone decides.
No kernel may reach another device: no remote copies, remote signals or barrier semaphores. Data moves between devices by JAX's collectives and lax.ppermute only.
A program may use at most 128 MiB of HBM per device.

v0:
```python
import functools
import math

import jax
import jax.numpy as jnp
import numpy as np
from jax import lax
from jax.experimental import pallas as pl
from jax.experimental.pallas import tpu as pltpu
from jax.sharding import PartitionSpec as P

VMEM_LIMIT = 48 * 1024 * 1024
VMEM_WIDE = 60 * 1024 * 1024
SIDE = 4


def split_pair(table):
    high = table.astype(np.float32).astype(jnp.bfloat16)
    low = (table - high.astype(np.float64)).astype(np.float32).astype(jnp.bfloat16)
    return high, low


def transform_tables(blocks, width, rows):
    length = 2 * blocks * rows
    kept = blocks + 1
    padded = -(-kept * width // 16) * 16
    k1 = np.arange(kept)
    block = np.arange(blocks)
    angle = 2.0 * np.pi * ((k1[:, None] * block[None, :]) % (2 * blocks)) / (2 * blocks)
    eye = np.eye(width)

    def spread(matrix):
        wide = np.kron(matrix, eye)
        return np.pad(wide, ((0, padded - wide.shape[0]), (0, 0)))

    mix = np.concatenate([spread(np.cos(angle)), spread(-np.sin(angle))], axis=0)
    weight = np.where((k1 == 0) | (k1 == blocks), 1.0, 2.0)[:, None] / length
    unmix = np.concatenate(
        [spread(weight * np.cos(angle)), spread(-weight * np.sin(angle))], axis=0
    ).T
    row = np.arange(rows)
    turn = 2.0 * np.pi * ((k1[:, None] * row[None, :]) % length) / length
    turn = np.pad(np.repeat(turn, width, axis=0), ((0, padded - kept * width), (0, 0)))
    inner = 2.0 * np.pi * ((row[:, None] * row[None, :]) % rows) / rows
    cos, sin = np.cos(inner), np.sin(inner)
    forward = np.block([[cos, -sin], [sin, cos]])
    inverse = np.block([[cos, sin], [-sin, cos]])
    turn = np.concatenate([np.cos(turn), np.sin(turn)], axis=1).astype(np.float32)
    return [split_pair(matrix) for matrix in (mix, forward, inverse, unmix)], turn


def packed(tables):
    width = max(min(high.shape) for high, _ in tables)
    slabs, places, first = [], [], 0
    for pair in tables:
        for table in pair:
            pieces = []
            for start in range(0, table.shape[1], width):
                slab = table[:, start : start + width]
                pieces.append((first, slab.shape))
                first += slab.shape[0]
                slabs.append(np.pad(slab, ((0, 0), (0, width - slab.shape[1]))))
            places.append(pieces)
    return np.concatenate(slabs, axis=0), places


def halves(value):
    high = value.astype(jnp.bfloat16)
    return high, (value - high.astype(jnp.float32)).astype(jnp.bfloat16)


def dot32(left, right):
    (lh, ll), (rh, rl) = left, right
    dot = functools.partial(jnp.dot, preferred_element_type=jnp.float32)
    return dot(lh, rh) + (dot(lh, rl) + dot(ll, rh))


def layout_kernel(x_ref, *moved_refs):
    far, _, _, part = moved_refs[0].shape
    device = lax.axis_index("seq")
    for chip in range(far * SIDE):
        distance = (chip // SIDE) ^ (device // (2 * SIDE))
        near = (chip % SIDE) ^ ((device // 2) % SIDE)
        for which, moved_ref in enumerate(moved_refs):

            @pl.when(near == which)
            def _():
                for c in range(2):
                    first = (2 * chip + c) * part
                    moved_ref[distance, (device % 2) ^ c] = x_ref[:, first : first + part].astype(
                        jnp.float32
                    )


def project_kernel(scaling, x_ref, w_ref, taps_ref, go_ref, *refs):
    sig_ref, kv_ref, acc = refs[-3:]
    step = pl.program_id(0)
    product = jnp.dot(x_ref[...], w_ref[...], preferred_element_type=jnp.float32)

    @pl.when(step == 0)
    def _():
        acc[...] = product

    @pl.when(step > 0)
    def _():
        acc[...] += product

    @pl.when(step == pl.num_programs(0) - 1)
    def _():
        count, _, width, _ = sig_ref.shape
        channels = count * width
        projected = acc[...].astype(jnp.bfloat16).astype(jnp.float32).T
        query = projected[:channels]
        key = projected[channels : 2 * channels]
        value = projected[2 * channels :]
        go = go_ref[...].astype(jnp.float32).T
        signals = ((taps_ref[...] * scaling).T, key * value, go * query)
        for which, signal in enumerate(signals):
            for owner in range(count):
                sig_ref[owner, which] = signal[owner * width : (owner + 1) * width]
        kv_ref[0] = go
        kv_ref[1] = value
        kv_ref[2] = key


def conv_kernel(places, x_ref, table_ref, turn_ref, *refs):
    y_ref, flat = refs[-2:]
    blocks, _, width, rows = x_ref.shape

    def table(which):
        slabs = [table_ref[at : at + shape[0], : shape[1]] for at, shape in places[which]]
        return slabs[0] if len(slabs) == 1 else jnp.concatenate(slabs, axis=1)

    m_h, m_l, f_h, f_l, i_h, i_l, u_h, u_l = [functools.partial(table, w) for w in range(8)]
    for p in range(blocks):
        for s in range(3):
            flat[p * width : (p + 1) * width, s * rows : (s + 1) * rows] = x_ref[p, s]
    turn_re, turn_im = turn_ref[:, :rows], turn_ref[:, rows:]
    count = turn_re.shape[0]
    mixed = dot32((m_h(), m_l()), halves(flat[...]))
    turned = []
    for s in range(3):
        re = mixed[:count, s * rows : (s + 1) * rows]
        im = mixed[count:, s * rows : (s + 1) * rows]
        turned.append(
            jnp.concatenate([re * turn_re + im * turn_im, im * turn_re - re * turn_im], axis=1)
        )
    spectrum = dot32(halves(jnp.concatenate(turned, axis=0)), (f_h(), f_l()))
    (k_re, k_im), (g_re, g_im), (b_re, b_im) = [
        (spectrum[s * count : (s + 1) * count, :rows], spectrum[s * count : (s + 1) * count, rows:])
        for s in range(3)
    ]
    products = jnp.concatenate(
        [
            jnp.concatenate([k_re * g_re - k_im * g_im, k_re * g_im + k_im * g_re], axis=1),
            jnp.concatenate([k_re * b_re + k_im * b_im, k_re * b_im - k_im * b_re], axis=1),
            jnp.concatenate([b_re * g_re + b_im * g_im, b_im * g_re - b_re * g_im], axis=1),
        ],
        axis=0,
    )
    back = dot32(halves(products), (i_h(), i_l()))
    parts_re, parts_im = [], []
    for s in range(3):
        re = back[s * count : (s + 1) * count, :rows]
        im = back[s * count : (s + 1) * count, rows:]
        parts_re.append(re * turn_re - im * turn_im)
        parts_im.append(im * turn_re + re * turn_im)
    stacked = jnp.concatenate(
        [jnp.concatenate(parts_re, axis=1), jnp.concatenate(parts_im, axis=1)], axis=0
    )
    result = dot32((u_h(), u_l()), halves(stacked))
    for p in range(blocks):
        for s in range(3):
            y_ref[p, s] = result[p * width : (p + 1) * width, s * rows : (s + 1) * rows]


def gate_first_kernel(y_ref, kv_ref, *refs):
    gp_ref, sent_ref, flat = refs[-3:]
    count, _, width, _ = y_ref.shape
    for owner in range(count):
        flat[owner * width : (owner + 1) * width] = y_ref[owner, 0]
    rounded = (kv_ref[0] * flat[...]).T.astype(jnp.bfloat16)
    gp_ref[...] = rounded
    sent_ref[...] = rounded.astype(jnp.float32)


def gate_rest_kernel(scaling, y_ref, kv_ref, first_ref, *refs):
    gp_ref, sent_ref, taps_ref, flat = refs[-4:]
    count, _, width, _ = y_ref.shape
    channels = count * width
    for s in range(2):
        for owner in range(count):
            flat[s, owner * width : (owner + 1) * width] = y_ref[owner, s + 1]
    gp_ref[:, :channels] = first_ref[...]
    for index in range(2):
        rounded = (kv_ref[index + 1] * flat[0]).T.astype(jnp.bfloat16)
        gp_ref[:, (index + 1) * channels : (index + 2) * channels] = rounded
        sent_ref[:, index * channels : (index + 1) * channels] = rounded.astype(jnp.float32)
    taps_ref[...] = flat[1].T * scaling


def turn_kernel(*refs):
    x_refs, out_refs = refs[:SIDE], refs[SIDE:]
    far, _, rows, part = x_refs[0].shape
    for which, x_ref in enumerate(x_refs):
        for core, out_ref in enumerate(out_refs):
            for f in range(far):
                out_ref[f * part : (f + 1) * part, which * rows : (which + 1) * rows] = (
                    x_ref[f, core].T.astype(jnp.bfloat16)
                )


def joined(gp_refs):
    return jnp.concatenate([gp_ref[...].astype(jnp.bfloat16) for gp_ref in gp_refs], axis=0)


def other_kernel(x_ref, *refs):
    gp_refs, out_ref = refs[:SIDE], refs[-1]
    out_ref[...] = jnp.dot(x_ref[...], joined(gp_refs), preferred_element_type=jnp.float32)


def own_kernel(x_ref, *refs):
    gp_refs, add_ref, out_refs = refs[:SIDE], refs[SIDE], refs[SIDE + 1 :]
    gp = joined(gp_refs)
    part = out_refs[0].shape[0]
    for which, out_ref in enumerate(out_refs):
        span = slice(which * part, (which + 1) * part)
        product = jnp.dot(x_ref[span], gp, preferred_element_type=jnp.float32)
        out_ref[...] = product + add_ref[span]


def sum_kernel(scaling, groups, *refs):
    *in_refs, out_ref = refs
    terms = len(in_refs) // groups
    first = 0
    for group in range(groups):
        total = in_refs[group * terms][...]
        for in_ref in in_refs[group * terms + 1 : (group + 1) * terms]:
            total = total + in_ref[...]
        out_ref[:, first : first + total.shape[1]] = total * scaling
        first += total.shape[1]


def per_device(inputs, in_weight, filter_taps, grad_out):
    rows, depth = inputs.shape
    channels = filter_taps.shape[1]
    columns = in_weight.shape[1]
    blocks = lax.axis_size("seq")
    width = channels // blocks
    part = depth // blocks
    far = blocks // (2 * SIDE)
    chunk = min(1024, depth)
    steps = depth // chunk
    scaling = 1.0 / math.sqrt(rows * blocks)
    f32, bf16 = jnp.float32, jnp.bfloat16
    params = pltpu.CompilerParams(vmem_limit_bytes=VMEM_LIMIT)
    wide = pltpu.CompilerParams(vmem_limit_bytes=VMEM_WIDE)

    def shaped(*shape, dtype=f32):
        return jax.ShapeDtypeStruct(shape, dtype)

    def exchange(value, flip):
        return lax.ppermute(value, "seq", [(i, i ^ flip) for i in range(blocks)])

    def gather(value):
        near, far_one = exchange(value, 2), exchange(value, 4)
        return [value, near, far_one, exchange(far_one, 2)]

    anywhere = pl.BlockSpec(memory_space=pl.ANY)
    inside = pl.BlockSpec(memory_space=pltpu.VMEM)
    moved = pl.pallas_call(
        layout_kernel,
        out_shape=[shaped(far, 2, rows, part)] * SIDE,
        compiler_params=wide,
    )(inputs)
    held = [moved[0]] + [exchange(moved[k], 2 * k) for k in range(1, SIDE)]
    signals, gates = pl.pallas_call(
        functools.partial(project_kernel, scaling),
        grid=(steps,),
        in_specs=[
            pl.BlockSpec((rows, chunk), lambda i: (0, i)),
            pl.BlockSpec((chunk, columns), lambda i: (i, 0)),
            pl.BlockSpec((rows, channels), lambda i: (0, 0)),
            pl.BlockSpec((rows, channels), lambda i: (0, 0)),
        ],
        out_specs=[
            pl.BlockSpec((blocks, 3, width, rows), lambda i: (0, 0, 0, 0)),
            pl.BlockSpec((3, channels, rows), lambda i: (0, 0, 0)),
        ],
        out_shape=[shaped(blocks, 3, width, rows), shaped(3, channels, rows)],
        scratch_shapes=[pltpu.VMEM((rows, columns), f32)],
        compiler_params=wide,
        cost_estimate=pl.CostEstimate(
            flops=2 * rows * depth * columns,
            bytes_accessed=2 * depth * (rows + columns),
            transcendentals=0,
        ),
    )(inputs, in_weight, filter_taps, grad_out)

    signals = lax.all_to_all(signals, "seq", split_axis=0, concat_axis=0, tiled=True)
    pairs, turn = transform_tables(blocks, width, rows)
    table, places = packed(pairs)
    results = pl.pallas_call(
        functools.partial(conv_kernel, places),
        in_specs=[inside] * 3 + [anywhere] * 2,
        out_shape=shaped(blocks, 3, width, rows),
        scratch_shapes=[pltpu.VMEM((blocks * width, 3 * rows), f32)],
        compiler_params=wide,
    )(signals, jnp.asarray(table), jnp.asarray(turn), *held[1:3])
    results = lax.all_to_all(results, "seq", split_axis=0, concat_axis=0, tiled=True)
    first, sent_first = pl.pallas_call(
        gate_first_kernel,
        in_specs=[inside] * 2 + [anywhere],
        out_shape=[shaped(rows, channels, dtype=bf16), shaped(rows, channels)],
        scratch_shapes=[pltpu.VMEM((channels, rows), f32)],
        compiler_params=params,
    )(results, gates, held[3])
    gathered_first = gather(sent_first)
    grad_proj, sent_rest, grad_taps = pl.pallas_call(
        functools.partial(gate_rest_kernel, scaling),
        out_shape=[
            shaped(rows, columns, dtype=bf16),
            shaped(rows, 2 * channels),
            shaped(rows, channels),
        ],
        scratch_shapes=[pltpu.VMEM((2, channels, rows), f32)],
        compiler_params=params,
    )(results, gates, first)
    gathered_rest = gather(sent_rest)
    turned = pl.pallas_call(
        turn_kernel,
        out_shape=[shaped(far * part, SIDE * rows, dtype=bf16)] * 2,
        compiler_params=params,
        cost_estimate=pl.CostEstimate(
            flops=0, bytes_accessed=10 * SIDE * far * rows * part, transcendentals=0
        ),
    )(*held)
    grad_inputs = lax.dot_general(
        grad_proj, in_weight, (((1,), (1,)), ((), ())), preferred_element_type=f32
    ).astype(bf16)
    terms = []
    for gathered in (gathered_first, gathered_rest):
        cols = gathered[0].shape[1]
        cost = pl.CostEstimate(
            flops=2 * far * part * SIDE * rows * cols,
            bytes_accessed=4 * far * part * cols,
            transcendentals=0,
        )
        other = pl.pallas_call(
            other_kernel,
            in_specs=[inside] * (1 + SIDE) + [anywhere] * len(terms[1:]),
            out_shape=shaped(far * part, cols),
            compiler_params=params,
            cost_estimate=cost,
        )(turned[1], *gathered, *terms[1:])
        kept, *leaving = pl.pallas_call(
            own_kernel,
            out_shape=[shaped(part, cols)] * far,
            compiler_params=params,
            cost_estimate=cost,
        )(turned[0], *gathered, exchange(other, 1))
        terms += [kept] + [exchange(v, 2 * SIDE * (k + 1)) for k, v in enumerate(leaving)]
    grad_weight = pl.pallas_call(
        functools.partial(sum_kernel, scaling, 2),
        out_shape=shaped(part, columns),
        compiler_params=params,
    )(*terms)
    return grad_inputs, grad_weight, grad_taps


def solution(mesh):
    in_specs = (P(("grp", "seq"), None), P(), P("seq", None), P(("grp", "seq"), None))
    out_specs = (P(("grp", "seq"), None), P(("grp", "seq"), None), P(("grp", "seq"), None))
    return jax.shard_map(
        per_device, mesh=mesh, in_specs=in_specs, out_specs=out_specs, check_vma=False
    )
```

profile of v0, /device:TPU:0, one launch (start us, length us, event | category | flops | bytes accessed | tf_op | source)
XLA Modules:
  0.0 133.4 jit_solution(8747651509425731438)
XLA Ops:
  0.6 5.7 %shard_map.85 = (f32[16,3,16,128]{3,2,1,0:T(8,128)}, f32[3,256,128]{2,1,0:T(8,128)}) custom-call(bf16[128,4096]{1,0:T(8,128)(2,1)} %x_ref.3, bf16[4096,768]{1,0:T(8,128)(2,1)} %w_ref.1, f32[128,256]{1,0:T(8,128)} %taps_ref.1, bf16[128,256]{1,0:T(8,128)(2,1)} %go_ref.1), custom_call_target="tpu_custom_call" | custom-call | flops 805306368 | bytes 7340032 | tf_op jit(solution)/shard_map/pallas_call | solution.py:277
  6.3 7.5 %all-to-all-start = ((f32[16,3,16,128]{3,2,1,0:T(8,128)}), f32[16,3,16,128]{3,2,1,0:T(8,128)S(1)}, u32[]{:S(2)}, u32[]{:S(2)}) async-start(f32[16,3,16,128]{3,2,1,0:T(8,128)} %get-tuple-element.20), calls=%async_computation | async-start | bytes 786432 | tf_op jit(solution)/shard_map/all_to_all | solution.py:300
  13.8 2.9 %shard_map.86 = (f32[2,2,128,256]{3,2,1,0:T(8,128)}, f32[2,2,128,256]{3,2,1,0:T(8,128)}, f32[2,2,128,256]{3,2,1,0:T(8,128)}, f32[2,2,128,256]{3,2,1,0:T(8,128)}) custom-call(bf16[128,4096]{1,0:T(8,128)(2,1)} %x_ref.3), custom_call_target="tpu_custom_call" | custom-call | tf_op jit(solution)/shard_map/pallas_call | solution.py:271
  16.7 1.9 %collective-permute-start = (f32[2,2,128,256]{3,2,1,0:T(8,128)}, f32[2,2,128,256]{3,2,1,0:T(8,128)S(1)}, u32[]{:S(2)}, u32[]{:S(2)}) collective-permute-start(f32[2,2,128,256]{3,2,1,0:T(8,128)} %get-tuple-element.21), channel_id=1, source_target_pairs={{0,2},{1,3},{2,0},{3,1},{4,6},{5,7},{6,4},{7,5},{8,10},{9,11},{10,... | collective-permute-start | bytes 1572872 | tf_op jit(solution)/shard_map/ppermute | solution.py:263
  18.6 1.5 %collective-permute-start.1 = (f32[2,2,128,256]{3,2,1,0:T(8,128)}, f32[2,2,128,256]{3,2,1,0:T(8,128)S(1)}, u32[]{:S(2)}, u32[]{:S(2)}) collective-permute-start(f32[2,2,128,256]{3,2,1,0:T(8,128)} %get-tuple-element.22), channel_id=1, source_target_pairs={{0,4},{1,5},{2,6},{3,7},{4,0},{5,1},{6,2},{7,3},{8,12},{9,13},{10,... | collective-permute-start | bytes 1572872 | tf_op jit(solution)/shard_map/ppermute | solution.py:263
  20.0 12.9 %collective-permute-done.refs_0_.refs_1_ = f32[2,2,128,256]{3,2,1,0:T(8,128)S(1)} collective-permute-done((f32[2,2,128,256]{3,2,1,0:T(8,128)}, f32[2,2,128,256]{3,2,1,0:T(8,128)S(1)}, u32[]{:S(2)}, u32[]{:S(2)}) %collective-permute-start) | collective-permute-done | bytes 524320 | tf_op jit(solution)/shard_map/ppermute | solution.py:263
  33.0 1.7 %collective-permute-done.1.refs_1_.refs_2_ = f32[2,2,128,256]{3,2,1,0:T(8,128)S(1)} collective-permute-done((f32[2,2,128,256]{3,2,1,0:T(8,128)}, f32[2,2,128,256]{3,2,1,0:T(8,128)S(1)}, u32[]{:S(2)}, u32[]{:S(2)}) %collective-permute-start.1) | collective-permute-done | bytes 524320 | tf_op jit(solution)/shard_map/ppermute | solution.py:263
  34.7 0.0 all-to-all-done.x_ref
  34.7 0.0 copy-done
  34.7 0.8 copy-done.2
  35.5 0.7 copy-done.6
  36.3 5.0 %shard_map.87 = f32[16,3,16,128]{3,2,1,0:T(8,128)} custom-call(f32[16,3,16,128]{3,2,1,0:T(8,128)} %copy-done.6, bf16[3648,256]{1,0:T(8,128)(2,1)} %constant.4.clone.table_ref, f32[272,256]{1,0:T(8,128)} %constant.5.clone.turn_ref, f32[2,2,128,256]{3,2,1,0:T(8,128)} %copy-done, f32[2,2,128,256]{3,2,1,0:T(8,128)} %copy-done.2), custom_call_target="tpu_custom_call" | custom-call | tf_op jit(solution)/shard_map/pallas_call | solution.py:303
  41.2 4.7 %all-to-all-start.1 = ((f32[16,3,16,128]{3,2,1,0:T(8,128)}), f32[16,3,16,128]{3,2,1,0:T(8,128)S(1)}, u32[]{:S(2)}, u32[]{:S(2)}) async-start(f32[16,3,16,128]{3,2,1,0:T(8,128)} %shard_map.87), calls=%async_computation.1 | async-start | bytes 786432 | tf_op jit(solution)/shard_map/all_to_all | solution.py:310
  46.0 2.8 %collective-permute-start.2 = (f32[2,2,128,256]{3,2,1,0:T(8,128)}, f32[2,2,128,256]{3,2,1,0:T(8,128)S(1)}, u32[]{:S(2)}, u32[]{:S(2)}) collective-permute-start(f32[2,2,128,256]{3,2,1,0:T(8,128)} %get-tuple-element.24), channel_id=1, source_target_pairs={{0,6},{1,7},{2,4},{3,5},{4,2},{5,3},{6,0},{7,1},{8,14},{9,15},{10,... | collective-permute-start | bytes 1572872 | tf_op jit(solution)/shard_map/ppermute | solution.py:263
  48.8 18.8 %collective-permute-done.2.refs_0_.refs_3_ = f32[2,2,128,256]{3,2,1,0:T(8,128)S(1)} collective-permute-done((f32[2,2,128,256]{3,2,1,0:T(8,128)}, f32[2,2,128,256]{3,2,1,0:T(8,128)S(1)}, u32[]{:S(2)}, u32[]{:S(2)}) %collective-permute-start.2) | collective-permute-done | bytes 524320 | tf_op jit(solution)/shard_map/ppermute | solution.py:263
  67.6 0.0 all-to-all-done.1.y_ref
  67.6 0.0 copy-done.4
  67.6 0.1 shard_map.88
  67.7 1.3 collective-permute-start.4
  69.0 0.9 collective-permute-start.3
  69.9 2.9 %collective-permute-done.4.refs_2_ = f32[128,256]{1,0:T(8,128)S(1)} collective-permute-done((f32[128,256]{1,0:T(8,128)S(1)}, f32[128,256]{1,0:T(8,128)S(1)}, u32[]{:S(2)}, u32[]{:S(2)}) %collective-permute-start.4) | collective-permute-done | bytes 131104 | tf_op jit(solution)/shard_map/ppermute | solution.py:263
  72.8 0.7 collective-permute-start.5
  73.5 1.0 copy-done.1
  74.5 1.0 copy-done.3
  75.5 0.3 shard_map.90
  75.9 0.0 collective-permute-done.3.refs_1_
  75.9 1.8 %collective-permute-done.5.refs_3_ = f32[128,256]{1,0:T(8,128)S(1)} collective-permute-done((f32[128,256]{1,0:T(8,128)S(1)}, f32[128,256]{1,0:T(8,128)S(1)}, u32[]{:S(2)}, u32[]{:S(2)}) %collective-permute-start.5) | collective-permute-done | bytes 131104 | tf_op jit(solution)/shard_map/ppermute | solution.py:263
  77.7 0.3 shard_map.91
  78.0 0.1 collective-permute-start.6
  78.1 0.8 shard_map.89
  78.9 1.2 collective-permute-start.9
  80.1 1.2 collective-permute-start.8
  81.3 6.3 %collective-permute-done.9.refs_2_ = f32[128,512]{1,0:T(8,128)S(1)} collective-permute-done((f32[128,512]{1,0:T(8,128)S(1)}, f32[128,512]{1,0:T(8,128)S(1)}, u32[]{:S(2)}, u32[]{:S(2)}) %collective-permute-start.9) | collective-permute-done | bytes 262176 | tf_op jit(solution)/shard_map/ppermute | solution.py:263
  87.6 0.7 collective-permute-start.10
  88.3 0.0 collective-permute-done.6.refs_4_
  88.3 0.3 shard_map.92
  88.6 2.6 %collective-permute-start.7 = (f32[256,256]{1,0:T(8,128)S(1)}, f32[256,256]{1,0:T(8,128)S(1)}, u32[]{:S(2)}, u32[]{:S(2)}) collective-permute-start(f32[256,256]{1,0:T(8,128)S(1)} %get-tuple-element.32), channel_id=1, source_target_pairs={{0,8},{1,9},{2,10},{3,11},{4,12},{5,13},{6,14},{7,15},{8,0},{9,1},... | collective-permute-start | bytes 786440 | tf_op jit(solution)/shard_map/ppermute | solution.py:263
  91.2 0.0 collective-permute-done.8.refs_1_
  91.2 4.4 %collective-permute-done.10.refs_3_ = f32[128,512]{1,0:T(8,128)S(1)} collective-permute-done((f32[128,512]{1,0:T(8,128)S(1)}, f32[128,512]{1,0:T(8,128)S(1)}, u32[]{:S(2)}, u32[]{:S(2)}) %collective-permute-start.10) | collective-permute-done | bytes 262176 | tf_op jit(solution)/shard_map/ppermute | solution.py:263
  95.6 7.3 %collective-permute-done.7.refs_4_.refs_1_ = f32[256,256]{1,0:T(8,128)S(1)} collective-permute-done((f32[256,256]{1,0:T(8,128)S(1)}, f32[256,256]{1,0:T(8,128)S(1)}, u32[]{:S(2)}, u32[]{:S(2)}) %collective-permute-start.7) | collective-permute-done | bytes 262176 | tf_op jit(solution)/shard_map/ppermute | solution.py:263
  102.8 0.4 shard_map.93
  103.3 0.1 collective-permute-start.11
  103.4 2.6 %collective-permute-done.11.refs_4_ = f32[512,512]{1,0:T(8,128)S(1)} collective-permute-done((f32[512,512]{1,0:T(8,128)S(1)}, f32[512,512]{1,0:T(8,128)S(1)}, u32[]{:S(2)}, u32[]{:S(2)}) %collective-permute-start.11) | collective-permute-done | bytes 1048608 | tf_op jit(solution)/shard_map/ppermute | solution.py:263
  106.0 0.4 shard_map.94
  106.5 0.1 collective-permute-start.12
  106.5 5.9 %convolution_convert_fusion = bf16[128,4096]{1,0:T(8,128)(2,1)} fusion(bf16[128,768]{1,0:T(8,128)(2,1)S(1)} %get-tuple-element.26, bf16[4096,768]{1,0:T(8,128)(2,1)} %w_ref.1), kind=kOutput, calls=%fused_computation | convolution fusion | flops 805830656 | bytes 7536640 | tf_op jit(solution)/shard_map/dot_general | solution.py:338
  112.4 20.0 %collective-permute-done.12.refs_3_ = f32[256,512]{1,0:T(8,128)S(1)} collective-permute-done((f32[256,512]{1,0:T(8,128)S(1)}, f32[256,512]{1,0:T(8,128)S(1)}, u32[]{:S(2)}, u32[]{:S(2)}) %collective-permute-start.12) | collective-permute-done | bytes 524320 | tf_op jit(solution)/shard_map/ppermute | solution.py:263
  132.4 1.0 shard_map.95
  (8 shorter events, 0.0 us)
Async XLA Ops:
  6.3 61.3 %copy-start.4 = (f32[3,256,128]{2,1,0:T(8,128)S(1)}, f32[3,256,128]{2,1,0:T(8,128)}, u32[]{:S(2)}) copy-start(f32[3,256,128]{2,1,0:T(8,128)} %get-tuple-element.23.kv_ref) | copy-start | bytes 1179652
  6.3 28.4 %all-to-all-start = ((f32[16,3,16,128]{3,2,1,0:T(8,128)}), f32[16,3,16,128]{3,2,1,0:T(8,128)S(1)}, u32[]{:S(2)}, u32[]{:S(2)}) async-start(f32[16,3,16,128]{3,2,1,0:T(8,128)} %get-tuple-element.20), calls=%async_computation | async-start | bytes 786432 | tf_op jit(solution)/shard_map/all_to_all | solution.py:300
  16.7 56.8 %copy-start.5 = (f32[2,2,128,256]{3,2,1,0:T(8,128)S(1)}, f32[2,2,128,256]{3,2,1,0:T(8,128)}, u32[]{:S(2)}) copy-start(f32[2,2,128,256]{3,2,1,0:T(8,128)} %get-tuple-element.27.refs_0_) | copy-start | bytes 1572868
  16.7 16.3 %collective-permute-start = (f32[2,2,128,256]{3,2,1,0:T(8,128)}, f32[2,2,128,256]{3,2,1,0:T(8,128)S(1)}, u32[]{:S(2)}, u32[]{:S(2)}) collective-permute-start(f32[2,2,128,256]{3,2,1,0:T(8,128)} %get-tuple-element.21), channel_id=1, source_target_pairs={{0,2},{1,3},{2,0},{3,1},{4,6},{5,7},{6,4},{7,5},{8,10},{9,11},{10,... | collective-permute-start | bytes 1572872 | tf_op jit(solution)/shard_map/ppermute | solution.py:263
  18.6 16.1 %collective-permute-start.1 = (f32[2,2,128,256]{3,2,1,0:T(8,128)}, f32[2,2,128,256]{3,2,1,0:T(8,128)S(1)}, u32[]{:S(2)}, u32[]{:S(2)}) collective-permute-start(f32[2,2,128,256]{3,2,1,0:T(8,128)} %get-tuple-element.22), channel_id=1, source_target_pairs={{0,4},{1,5},{2,6},{3,7},{4,0},{5,1},{6,2},{7,3},{8,12},{9,13},{10,... | collective-permute-start | bytes 1572872 | tf_op jit(solution)/shard_map/ppermute | solution.py:263
  33.0 1.7 %copy-start = (f32[2,2,128,256]{3,2,1,0:T(8,128)}, f32[2,2,128,256]{3,2,1,0:T(8,128)S(1)}, u32[]{:S(2)}) copy-start(f32[2,2,128,256]{3,2,1,0:T(8,128)S(1)} %collective-permute-done.refs_0_.refs_1_) | copy-start | bytes 1572868
  34.7 0.8 copy-start.2
  35.5 0.7 copy-start.6
  41.2 26.3 %all-to-all-start.1 = ((f32[16,3,16,128]{3,2,1,0:T(8,128)}), f32[16,3,16,128]{3,2,1,0:T(8,128)S(1)}, u32[]{:S(2)}, u32[]{:S(2)}) async-start(f32[16,3,16,128]{3,2,1,0:T(8,128)} %shard_map.87), calls=%async_computation.1 | async-start | bytes 786432 | tf_op jit(solution)/shard_map/all_to_all | solution.py:310
  46.0 21.6 %collective-permute-start.2 = (f32[2,2,128,256]{3,2,1,0:T(8,128)}, f32[2,2,128,256]{3,2,1,0:T(8,128)S(1)}, u32[]{:S(2)}, u32[]{:S(2)}) collective-permute-start(f32[2,2,128,256]{3,2,1,0:T(8,128)} %get-tuple-element.24), channel_id=1, source_target_pairs={{0,6},{1,7},{2,4},{3,5},{4,2},{5,3},{6,0},{7,1},{8,14},{9,15},{10,... | collective-permute-start | bytes 1572872 | tf_op jit(solution)/shard_map/ppermute | solution.py:263
  67.7 5.1 %collective-permute-start.4 = (f32[128,256]{1,0:T(8,128)S(1)}, f32[128,256]{1,0:T(8,128)S(1)}, u32[]{:S(2)}, u32[]{:S(2)}) collective-permute-start(f32[128,256]{1,0:T(8,128)S(1)} %get-tuple-element.29.refs_0_), channel_id=1, source_target_pairs={{0,4},{1,5},{2,6},{3,7},{4,0},{5,1},{6,2},{7,3},{8,12},{9,13},{10,... | collective-permute-start | bytes 393224 | tf_op jit(solution)/shard_map/ppermute | solution.py:263
  69.0 6.9 %collective-permute-start.3 = (f32[128,256]{1,0:T(8,128)S(1)}, f32[128,256]{1,0:T(8,128)S(1)}, u32[]{:S(2)}, u32[]{:S(2)}) collective-permute-start(f32[128,256]{1,0:T(8,128)S(1)} %get-tuple-element.29.refs_0_), channel_id=1, source_target_pairs={{0,2},{1,3},{2,0},{3,1},{4,6},{5,7},{6,4},{7,5},{8,10},{9,11},{10,... | collective-permute-start | bytes 393224 | tf_op jit(solution)/shard_map/ppermute | solution.py:263
  72.8 5.0 %collective-permute-start.5 = (f32[128,256]{1,0:T(8,128)S(1)}, f32[128,256]{1,0:T(8,128)S(1)}, u32[]{:S(2)}, u32[]{:S(2)}) collective-permute-start(f32[128,256]{1,0:T(8,128)S(1)} %collective-permute-done.4.refs_2_), channel_id=1, source_target_pairs={{0,2},{1,3},{2,0},{3,1},{4,6},{5,7},{6,4},{7,5},{8,10},{9,11},{10,... | collective-permute-start | bytes 393224 | tf_op jit(solution)/shard_map/ppermute | solution.py:263
  73.5 1.0 copy-start.1
  74.5 1.0 copy-start.3
  78.0 10.3 %collective-permute-start.6 = (f32[512,256]{1,0:T(8,128)S(1)}, f32[512,256]{1,0:T(8,128)S(1)}, u32[]{:S(2)}, u32[]{:S(2)}) collective-permute-start(f32[512,256]{1,0:T(8,128)S(1)} %shard_map.91), channel_id=1, source_target_pairs={{0,1},{1,0},{2,3},{3,2},{4,5},{5,4},{6,7},{7,6},{8,9},{9,8},{10,11... | collective-permute-start | bytes 1572872 | tf_op jit(solution)/shard_map/ppermute | solution.py:263
  78.9 8.7 %collective-permute-start.9 = (f32[128,512]{1,0:T(8,128)S(1)}, f32[128,512]{1,0:T(8,128)S(1)}, u32[]{:S(2)}, u32[]{:S(2)}) collective-permute-start(f32[128,512]{1,0:T(8,128)S(1)} %get-tuple-element.33.refs_0_), channel_id=1, source_target_pairs={{0,4},{1,5},{2,6},{3,7},{4,0},{5,1},{6,2},{7,3},{8,12},{9,13},{10,... | collective-permute-start | bytes 786440 | tf_op jit(solution)/shard_map/ppermute | solution.py:263
  80.1 11.1 %collective-permute-start.8 = (f32[128,512]{1,0:T(8,128)S(1)}, f32[128,512]{1,0:T(8,128)S(1)}, u32[]{:S(2)}, u32[]{:S(2)}) collective-permute-start(f32[128,512]{1,0:T(8,128)S(1)} %get-tuple-element.33.refs_0_), channel_id=1, source_target_pairs={{0,2},{1,3},{2,0},{3,1},{4,6},{5,7},{6,4},{7,5},{8,10},{9,11},{10,... | collective-permute-start | bytes 786440 | tf_op jit(solution)/shard_map/ppermute | solution.py:263
  87.6 7.9 %collective-permute-start.10 = (f32[128,512]{1,0:T(8,128)S(1)}, f32[128,512]{1,0:T(8,128)S(1)}, u32[]{:S(2)}, u32[]{:S(2)}) collective-permute-start(f32[128,512]{1,0:T(8,128)S(1)} %collective-permute-done.9.refs_2_), channel_id=1, source_target_pairs={{0,2},{1,3},{2,0},{3,1},{4,6},{5,7},{6,4},{7,5},{8,10},{9,11},{10,... | collective-permute-start | bytes 786440 | tf_op jit(solution)/shard_map/ppermute | solution.py:263
  88.6 14.2 %collective-permute-start.7 = (f32[256,256]{1,0:T(8,128)S(1)}, f32[256,256]{1,0:T(8,128)S(1)}, u32[]{:S(2)}, u32[]{:S(2)}) collective-permute-start(f32[256,256]{1,0:T(8,128)S(1)} %get-tuple-element.32), channel_id=1, source_target_pairs={{0,8},{1,9},{2,10},{3,11},{4,12},{5,13},{6,14},{7,15},{8,0},{9,1},... | collective-permute-start | bytes 786440 | tf_op jit(solution)/shard_map/ppermute | solution.py:263
  103.3 2.7 %collective-permute-start.11 = (f32[512,512]{1,0:T(8,128)S(1)}, f32[512,512]{1,0:T(8,128)S(1)}, u32[]{:S(2)}, u32[]{:S(2)}) collective-permute-start(f32[512,512]{1,0:T(8,128)S(1)} %shard_map.93), channel_id=1, source_target_pairs={{0,1},{1,0},{2,3},{3,2},{4,5},{5,4},{6,7},{7,6},{8,9},{9,8},{10,11... | collective-permute-start | bytes 3145736 | tf_op jit(solution)/shard_map/ppermute | solution.py:263
  106.5 26.0 %collective-permute-start.12 = (f32[256,512]{1,0:T(8,128)S(1)}, f32[256,512]{1,0:T(8,128)S(1)}, u32[]{:S(2)}, u32[]{:S(2)}) collective-permute-start(f32[256,512]{1,0:T(8,128)S(1)} %get-tuple-element.35), channel_id=1, source_target_pairs={{0,8},{1,9},{2,10},{3,11},{4,12},{5,13},{6,14},{7,15},{8,0},{9,1},... | collective-permute-start | bytes 1572872 | tf_op jit(solution)/shard_map/ppermute | solution.py:263
where the time goes:
time: 134 us; the launch traced here: 133 us
  waiting for transfers between devices  78.7 us (59%)
  starting transfers between devices  27.2 us (20%)
  Pallas kernels  17.2 us (13%)
  matrix products  5.9 us (4%)
  local copies, waits for them, and re-layouts  3.66 us (3%)
    ppermute x13, waiting for transfers between devices, exchange(): return lax.ppermute(value, 'seq', [(i, i ^ flip) for i in range(blocks)])  78.7 us
    ppermute x13, starting transfers between devices, exchange(): return lax.ppermute(value, 'seq', [(i, i ^ flip) for i in range(blocks)])  15 us
    all_to_all x1, starting transfers between devices, per_device(): lax.all_to_all(signals, 'seq', split_axis=0, concat_axis=0, tiled=True)  7.52 us
    dot_general x1, matrix products, per_device(): lax.dot_general(grad_proj, in_weight, (((1,), (1,)), ((), ())), preferred...  5.9 us
    pallas_call x1, Pallas kernels, per_device(): pl.pallas_call(functools.partial(project_kernel, scaling), grid=(steps,),...  5.66 us
    pallas_call x1, Pallas kernels, per_device(): pl.pallas_call(functools.partial(conv_kernel, places), in_specs=[inside]...  4.98 us
    all_to_all x1, starting transfers between devices, per_device(): lax.all_to_all(results, 'seq', split_axis=0, concat_axis=0, tiled=True)  4.72 us
    unnamed x14, local copies, waits for them, and re-layouts  3.66 us
  transfers between devices with their start and end apart: 15, of which 10 were waited for; matrix products, arithmetic and copies ran while one was open for 4% of the time, Pallas kernels for 3%

commit v1 on v0

--- a/solution.py
+++ b/solution.py
@@ -75,25 +75,34 @@
     return dot(lh, rh) + (dot(lh, rl) + dot(ll, rh))
 
 
-def layout_kernel(x_ref, *moved_refs):
-    far, _, _, part = moved_refs[0].shape
+def layout_kernel(x_ref, own_ref, y_ref, z_ref):
+    _, far, _, part = own_ref.shape
     device = lax.axis_index("seq")
+    places = {
+        (0, 0): (own_ref, 0),
+        (0, 1): (own_ref, 1),
+        (1, 0): (y_ref, 0),
+        (3, 0): (y_ref, 1),
+        (1, 1): (y_ref, 2),
+        (2, 1): (z_ref, 0),
+        (3, 1): (z_ref, 1),
+        (2, 0): (z_ref, 2),
+    }
     for chip in range(far * SIDE):
         distance = (chip // SIDE) ^ (device // (2 * SIDE))
         near = (chip % SIDE) ^ ((device // 2) % SIDE)
-        for which, moved_ref in enumerate(moved_refs):
-
-            @pl.when(near == which)
-            def _():
-                for c in range(2):
-                    first = (2 * chip + c) * part
-                    moved_ref[distance, (device % 2) ^ c] = x_ref[:, first : first + part].astype(
-                        jnp.float32
-                    )
+        for core in range(2):
+            first = (2 * chip + core) * part
+            flip = (device % 2) ^ core
+            for (side, cross), (out_ref, slot) in places.items():
+
+                @pl.when((near == side) & (flip == cross))
+                def _():
+                    out_ref[slot, distance] = x_ref[:, first : first + part].astype(jnp.float32)
 
 
 def project_kernel(scaling, x_ref, w_ref, taps_ref, go_ref, *refs):
-    sig_ref, kv_ref, acc = refs[-3:]
+    sig_ref, go_out_ref, key_ref, value_ref, acc = refs[-5:]
     step = pl.program_id(0)
     product = jnp.dot(x_ref[...], w_ref[...], preferred_element_type=jnp.float32)
 
@@ -118,9 +127,9 @@
         for which, signal in enumerate(signals):
             for owner in range(count):
                 sig_ref[owner, which] = signal[owner * width : (owner + 1) * width]
-        kv_ref[0] = go
-        kv_ref[1] = value
-        kv_ref[2] = key
+        go_out_ref[...] = go
+        key_ref[...] = key
+        value_ref[...] = value
 
 
 def conv_kernel(places, x_ref, table_ref, turn_ref, *refs):
@@ -174,39 +183,45 @@
             y_ref[p, s] = result[p * width : (p + 1) * width, s * rows : (s + 1) * rows]
 
 
-def gate_first_kernel(y_ref, kv_ref, *refs):
-    gp_ref, sent_ref, flat = refs[-3:]
+def gate_first_kernel(y_ref, go_ref, gp_ref, sent_ref, flat):
     count, _, width, _ = y_ref.shape
     for owner in range(count):
         flat[owner * width : (owner + 1) * width] = y_ref[owner, 0]
-    rounded = (kv_ref[0] * flat[...]).T.astype(jnp.bfloat16)
+    rounded = (go_ref[...] * flat[...]).T.astype(jnp.bfloat16)
     gp_ref[...] = rounded
     sent_ref[...] = rounded.astype(jnp.float32)
 
 
-def gate_rest_kernel(scaling, y_ref, kv_ref, first_ref, *refs):
-    gp_ref, sent_ref, taps_ref, flat = refs[-4:]
+def gate_rest_kernel(scaling, y_ref, key_ref, value_ref, first_ref, *refs):
+    gp_ref, sent_ref, taps_ref, flat = refs
     count, _, width, _ = y_ref.shape
     channels = count * width
     for s in range(2):
         for owner in range(count):
             flat[s, owner * width : (owner + 1) * width] = y_ref[owner, s + 1]
     gp_ref[:, :channels] = first_ref[...]
-    for index in range(2):
-        rounded = (kv_ref[index + 1] * flat[0]).T.astype(jnp.bfloat16)
+    for index, factor_ref in enumerate((value_ref, key_ref)):
+        rounded = (factor_ref[...] * flat[0]).T.astype(jnp.bfloat16)
         gp_ref[:, (index + 1) * channels : (index + 2) * channels] = rounded
         sent_ref[:, index * channels : (index + 1) * channels] = rounded.astype(jnp.float32)
     taps_ref[...] = flat[1].T * scaling
 
 
-def turn_kernel(*refs):
-    x_refs, out_refs = refs[:SIDE], refs[SIDE:]
-    far, _, rows, part = x_refs[0].shape
-    for which, x_ref in enumerate(x_refs):
-        for core, out_ref in enumerate(out_refs):
+def relay_kernel(x_ref, *refs):
+    refs[-1][...] = x_ref[...]
+
+
+def turn_kernel(own_ref, y_ref, z_ref, corner_own_ref, corner_other_ref, *out_refs):
+    _, far, rows, part = own_ref.shape
+    sources = (
+        ((own_ref, 0), (y_ref, 0), (z_ref, 2), (corner_own_ref, 0)),
+        ((own_ref, 1), (y_ref, 2), (z_ref, 0), (corner_other_ref, 0)),
+    )
+    for out_ref, chips in zip(out_refs, sources):
+        for which, (x_ref, slot) in enumerate(chips):
             for f in range(far):
                 out_ref[f * part : (f + 1) * part, which * rows : (which + 1) * rows] = (
-                    x_ref[f, core].T.astype(jnp.bfloat16)
+                    x_ref[slot, f].T.astype(jnp.bfloat16)
                 )
 
 
@@ -262,19 +277,17 @@
     def exchange(value, flip):
         return lax.ppermute(value, "seq", [(i, i ^ flip) for i in range(blocks)])
 
-    def gather(value):
-        near, far_one = exchange(value, 2), exchange(value, 4)
-        return [value, near, far_one, exchange(far_one, 2)]
-
     anywhere = pl.BlockSpec(memory_space=pl.ANY)
     inside = pl.BlockSpec(memory_space=pltpu.VMEM)
-    moved = pl.pallas_call(
+    own, to_y, to_z = pl.pallas_call(
         layout_kernel,
-        out_shape=[shaped(far, 2, rows, part)] * SIDE,
+        out_shape=[shaped(2, far, rows, part)] + [shaped(3, far, rows, part)] * 2,
         compiler_params=wide,
     )(inputs)
-    held = [moved[0]] + [exchange(moved[k], 2 * k) for k in range(1, SIDE)]
-    signals, gates = pl.pallas_call(
+    from_y, from_z = exchange(to_y, 2), exchange(to_z, 4)
+    corners = exchange(from_y[1:2], 4), exchange(from_z[1:2], 2)
+    held = (own, from_y, from_z) + corners
+    signals, gate_out, key, value = pl.pallas_call(
         functools.partial(project_kernel, scaling),
         grid=(steps,),
         in_specs=[
@@ -285,9 +298,9 @@
         ],
         out_specs=[
             pl.BlockSpec((blocks, 3, width, rows), lambda i: (0, 0, 0, 0)),
-            pl.BlockSpec((3, channels, rows), lambda i: (0, 0, 0)),
-        ],
-        out_shape=[shaped(blocks, 3, width, rows), shaped(3, channels, rows)],
+            ]
+        + [pl.BlockSpec((channels, rows), lambda i: (0, 0))] * 3,
+        out_shape=[shaped(blocks, 3, width, rows)] + [shaped(channels, rows)] * 3,
         scratch_shapes=[pltpu.VMEM((rows, columns), f32)],
         compiler_params=wide,
         cost_estimate=pl.CostEstimate(
@@ -305,17 +318,15 @@
         in_specs=[inside] * 3 + [anywhere] * 2,
         out_shape=shaped(blocks, 3, width, rows),
         scratch_shapes=[pltpu.VMEM((blocks * width, 3 * rows), f32)],
-        compiler_params=wide,
-    )(signals, jnp.asarray(table), jnp.asarray(turn), *held[1:3])
+        compiler_params=params,
+    )(signals, jnp.asarray(table), jnp.asarray(turn), *corners)
     results = lax.all_to_all(results, "seq", split_axis=0, concat_axis=0, tiled=True)
     first, sent_first = pl.pallas_call(
         gate_first_kernel,
-        in_specs=[inside] * 2 + [anywhere],
         out_shape=[shaped(rows, channels, dtype=bf16), shaped(rows, channels)],
         scratch_shapes=[pltpu.VMEM((channels, rows), f32)],
         compiler_params=params,
-    )(results, gates, held[3])
-    gathered_first = gather(sent_first)
+    )(results, gate_out)
     grad_proj, sent_rest, grad_taps = pl.pallas_call(
         functools.partial(gate_rest_kernel, scaling),
         out_shape=[
@@ -325,8 +336,7 @@
         ],
         scratch_shapes=[pltpu.VMEM((2, channels, rows), f32)],
         compiler_params=params,
-    )(results, gates, first)
-    gathered_rest = gather(sent_rest)
+    )(results, key, value, first)
     turned = pl.pallas_call(
         turn_kernel,
         out_shape=[shaped(far * part, SIDE * rows, dtype=bf16)] * 2,
@@ -339,8 +349,18 @@
         grad_proj, in_weight, (((1,), (1,)), ((), ())), preferred_element_type=f32
     ).astype(bf16)
     terms = []
-    for gathered in (gathered_first, gathered_rest):
-        cols = gathered[0].shape[1]
+    for block in (sent_first, sent_rest):
+        cols = block.shape[1]
+        from_far = exchange(block, 4)
+        relayed = from_far
+        if terms:
+            relayed = pl.pallas_call(
+                relay_kernel,
+                in_specs=[inside, anywhere],
+                out_shape=shaped(rows, cols),
+                compiler_params=params,
+            )(from_far, terms[0])
+        gathered = [block, exchange(block, 2), from_far, exchange(relayed, 2)]
         cost = pl.CostEstimate(
             flops=2 * far * part * SIDE * rows * cols,
             bytes_accessed=4 * far * part * cols,

time: 134 us -> 128 us (0.955)
  blocking collectives: 0 us -> 17 us
  waiting for transfers between devices: 78.7 us -> 67 us
  starting transfers between devices: 27.2 us -> 17.2 us
  matrix products: 5.9 us -> 3.11 us
  local copies, waits for them, and re-layouts: 3.66 us -> 5.31 us
    all_to_all x0 -> x1, blocking collectives: none -> 17 us  [per_device(): lax.all_to_all(results, 'seq', split_axis=0, concat_axis=0, tiled=True)]
    ppermute x13 -> x14, waiting for transfers between devices: 78.7 us -> 64.1 us  [exchange(): return lax.ppermute(value, 'seq', [(i, i ^ flip) for i in range(blocks)])]
    all_to_all x1 -> x0, starting transfers between devices: 4.72 us -> none  [per_device(): lax.all_to_all(results, 'seq', split_axis=0, concat_axis=0, tiled=True)]
    all_to_all x1, starting transfers between devices: 7.52 us -> 4.1 us  [per_device(): lax.all_to_all(signals, 'seq', split_axis=0, concat_axis=0, tiled=True)]
    all_to_all x1, waiting for transfers between devices: 0.01 us -> 2.84 us  [per_device(): lax.all_to_all(signals, 'seq', split_axis=0, concat_axis=0, tiled=True)]
    dot_general x1, matrix products: 5.9 us -> 3.11 us  [per_device(): lax.dot_general(grad_proj, in_weight, (((1,), (1,)), ((), ())), preferred...]
    pallas_call x1, Pallas kernels: 4.98 us -> 2.58 us  [per_device(): pl.pallas_call(functools.partial(conv_kernel, places), in_specs=[inside]...]
    slice x0 -> x2, local copies, waits for them, and re-layouts: none -> 2.39 us  [per_device(): corners = (exchange(from_y[1:2], 4), exchange(from_z[1:2], 2))]
  transfers between devices with their start and end apart: 15 -> 15, of which waited for: 10 -> 12; matrix products, arithmetic and copies ran while one was open for 4% -> 4% of each run, Pallas kernels for 3% -> 7%
where the time goes in v1:
time: 128 us; the launch traced here: 127 us
  waiting for transfers between devices  67 us (52%)
  starting transfers between devices  17.2 us (13%)
  blocking collectives  17 us (13%)
  Pallas kernels  16.8 us (13%)
  local copies, waits for them, and re-layouts  5.31 us (4%)
  matrix products  3.11 us (2%)
    ppermute x14, waiting for transfers between devices, exchange(): return lax.ppermute(value, 'seq', [(i, i ^ flip) for i in range(blocks)])  64.1 us
    all_to_all x1, blocking collectives, per_device(): lax.all_to_all(results, 'seq', split_axis=0, concat_axis=0, tiled=True)  17 us
    ppermute x14, starting transfers between devices, exchange(): return lax.ppermute(value, 'seq', [(i, i ^ flip) for i in range(blocks)])  13.1 us
    pallas_call x1, Pallas kernels, per_device(): pl.pallas_call(functools.partial(project_kernel, scaling), grid=(steps,),...  5.62 us
    all_to_all x1, starting transfers between devices, per_device(): lax.all_to_all(signals, 'seq', split_axis=0, concat_axis=0, tiled=True)  4.1 us
    pallas_call x1, Pallas kernels, per_device(): pl.pallas_call(layout_kernel, out_shape=[shaped(2, far, rows, part)] + [s...  3.6 us
    dot_general x1, matrix products, per_device(): lax.dot_general(grad_proj, in_weight, (((1,), (1,)), ((), ())), preferred...  3.11 us
    unnamed x16, local copies, waits for them, and re-layouts  2.92 us
  transfers between devices with their start and end apart: 15, of which 12 were waited for; matrix products, arithmetic and copies ran while one was open for 4% of the time, Pallas kernels for 7%

profile of v1, /device:TPU:0, one launch (start us, length us, event | category | flops | bytes accessed | tf_op | source)
XLA Modules:
  0.0 127.2 jit_solution(9355570311104856631)
XLA Ops:
  0.6 0.0 copy-start
  0.6 3.6 %shard_map.86 = (f32[2,2,128,256]{3,2,1,0:T(8,128)}, f32[3,2,128,256]{3,2,1,0:T(8,128)}, f32[3,2,128,256]{3,2,1,0:T(8,128)}) custom-call(bf16[128,4096]{1,0:T(8,128)(2,1)} %x_ref.3), custom_call_target="tpu_custom_call" | custom-call | tf_op jit(solution)/shard_map/pallas_call | solution.py:282
  4.2 3.0 %collective-permute-start = (f32[3,2,128,256]{3,2,1,0:T(8,128)}, f32[3,2,128,256]{3,2,1,0:T(8,128)S(1)}, u32[]{:S(2)}, u32[]{:S(2)}) collective-permute-start(f32[3,2,128,256]{3,2,1,0:T(8,128)} %get-tuple-element.22), channel_id=1, source_target_pairs={{0,2},{1,3},{2,0},{3,1},{4,6},{5,7},{6,4},{7,5},{8,10},{9,11},{10,... | collective-permute-start | bytes 2359304 | tf_op jit(solution)/shard_map/ppermute | solution.py:278
  7.2 1.6 %collective-permute-start.2 = (f32[3,2,128,256]{3,2,1,0:T(8,128)}, f32[3,2,128,256]{3,2,1,0:T(8,128)}, u32[]{:S(2)}, u32[]{:S(2)}) collective-permute-start(f32[3,2,128,256]{3,2,1,0:T(8,128)} %get-tuple-element.23), channel_id=1, source_target_pairs={{0,4},{1,5},{2,6},{3,7},{4,0},{5,1},{6,2},{7,3},{8,12},{9,13},{10,... | collective-permute-start | bytes 2359304 | tf_op jit(solution)/shard_map/ppermute | solution.py:278
  8.8 5.6 %shard_map.85 = (f32[16,3,16,128]{3,2,1,0:T(8,128)}, f32[256,128]{1,0:T(8,128)}, f32[256,128]{1,0:T(8,128)}, f32[256,128]{1,0:T(8,128)}) custom-call(bf16[128,4096]{1,0:T(8,128)(2,1)} %x_ref.3, bf16[4096,768]{1,0:T(8,128)(2,1)} %w_ref.1, f32[128,256]{1,0:T(8,128)} %taps_ref.1, bf16[128,256]{1,0:T(8,128)(2,1)} %go_ref.1), custom_call_target="tpu_custom_call" | custom-call | flops 805306368 | bytes 7340032 | tf_op jit(solution)/shard_map/pallas_call | solution.py:290
  14.4 4.1 %all-to-all-start = ((f32[16,3,16,128]{3,2,1,0:T(8,128)}), f32[16,3,16,128]{3,2,1,0:T(8,128)S(1)}, u32[]{:S(2)}, u32[]{:S(2)}) async-start(f32[16,3,16,128]{3,2,1,0:T(8,128)} %get-tuple-element.21), calls=%async_computation | async-start | bytes 786432 | tf_op jit(solution)/shard_map/all_to_all | solution.py:313
  18.5 8.0 %collective-permute-done.y_ref = f32[3,2,128,256]{3,2,1,0:T(8,128)S(1)} collective-permute-done((f32[3,2,128,256]{3,2,1,0:T(8,128)}, f32[3,2,128,256]{3,2,1,0:T(8,128)S(1)}, u32[]{:S(2)}, u32[]{:S(2)}) %collective-permute-start) | collective-permute-done | bytes 786464 | tf_op jit(solution)/shard_map/ppermute | solution.py:278
  26.5 0.7 slice.8
  27.2 1.6 %collective-permute-start.1 = (f32[1,2,128,256]{3,2,1,0:T(8,128)}, f32[1,2,128,256]{3,2,1,0:T(8,128)S(1)}, u32[]{:S(2)}, u32[]{:S(2)}) collective-permute-start(f32[1,2,128,256]{3,2,1,0:T(8,128)} %slice.8), channel_id=1, source_target_pairs={{0,4},{1,5},{2,6},{3,7},{4,0},{5,1},{6,2},{7,3},{8,12},{9,13},{10,... | collective-permute-start | bytes 786440 | tf_op jit(solution)/shard_map/ppermute | solution.py:278
  28.8 2.8 %collective-permute-done.2.z_ref = f32[3,2,128,256]{3,2,1,0:T(8,128)} collective-permute-done((f32[3,2,128,256]{3,2,1,0:T(8,128)}, f32[3,2,128,256]{3,2,1,0:T(8,128)}, u32[]{:S(2)}, u32[]{:S(2)}) %collective-permute-start.2) | collective-permute-done | bytes 786464 | tf_op jit(solution)/shard_map/ppermute | solution.py:278
  31.7 1.7 %slice.9 = f32[1,2,128,256]{3,2,1,0:T(8,128)} slice(f32[3,2,128,256]{3,2,1,0:T(8,128)} %collective-permute-done.2.z_ref), slice={[1:2], [0:2], [0:128], [0:256]} | slice | bytes 524288 | tf_op jit(solution)/shard_map/slice | solution.py:288
  33.3 0.0 collective-permute-start.3
  33.3 2.8 %all-to-all-done.x_ref = f32[16,3,16,128]{3,2,1,0:T(8,128)S(1)} async-done(((f32[16,3,16,128]{3,2,1,0:T(8,128)}), f32[16,3,16,128]{3,2,1,0:T(8,128)S(1)}, u32[]{:S(2)}, u32[]{:S(2)}) %all-to-all-start) | async-done | bytes 393248 | tf_op jit(solution)/shard_map/all_to_all | solution.py:313
  36.2 2.2 %collective-permute-done.1.refs_0_.corner_own_ref = f32[1,2,128,256]{3,2,1,0:T(8,128)S(1)} collective-permute-done((f32[1,2,128,256]{3,2,1,0:T(8,128)}, f32[1,2,128,256]{3,2,1,0:T(8,128)S(1)}, u32[]{:S(2)}, u32[]{:S(2)}) %collective-permute-start.1) | collective-permute-done | bytes 262176 | tf_op jit(solution)/shard_map/ppermute | solution.py:278
  38.3 1.7 %collective-permute-done.3.refs_1_.corner_other_ref = f32[1,2,128,256]{3,2,1,0:T(8,128)} collective-permute-done((f32[1,2,128,256]{3,2,1,0:T(8,128)}, f32[1,2,128,256]{3,2,1,0:T(8,128)}, u32[]{:S(2)}, u32[]{:S(2)}) %collective-permute-start.3) | collective-permute-done | bytes 262176 | tf_op jit(solution)/shard_map/ppermute | solution.py:278
  40.0 1.0 copy-done.2
  41.0 2.6 %shard_map.87 = f32[16,3,16,128]{3,2,1,0:T(8,128)S(1)} custom-call(f32[16,3,16,128]{3,2,1,0:T(8,128)S(1)} %all-to-all-done.x_ref, bf16[3648,256]{1,0:T(8,128)(2,1)S(1)} %copy-done, f32[272,256]{1,0:T(8,128)S(1)} %copy-done.2, f32[1,2,128,256]{3,2,1,0:T(8,128)S(1)} %collective-permute-done.1.refs_0_.corner_own_ref, ...), custom_call_target="tpu_custom_call" | custom-call | tf_op jit(solution)/shard_map/pallas_call | solution.py:316
  43.6 17.0 %all_to_all.10.y_ref = f32[16,3,16,128]{3,2,1,0:T(8,128)S(1)} all-to-all(f32[16,3,16,128]{3,2,1,0:T(8,128)S(1)} %shard_map.87), channel_id=1, replica_groups=mesh['grp'=2,'seq'=16] {'seq'}, dimensions={0} | all-to-all | bytes 786432 | tf_op jit(solution)/shard_map/all_to_all | solution.py:323
  60.6 0.9 copy-done.5
  61.5 0.1 shard_map.88
  61.6 0.8 collective-permute-start.5
  62.4 1.1 collective-permute-start.4
  63.4 3.7 %collective-permute-done.5.refs_2_ = f32[128,256]{1,0:T(8,128)S(1)} collective-permute-done((f32[128,256]{1,0:T(8,128)S(1)}, f32[128,256]{1,0:T(8,128)S(1)}, u32[]{:S(2)}, u32[]{:S(2)}) %collective-permute-start.5) | collective-permute-done | bytes 131104 | tf_op jit(solution)/shard_map/ppermute | solution.py:278
  67.2 0.8 collective-permute-start.6
  68.0 1.0 copy-done.1
  69.0 1.7 %shard_map.90 = (bf16[512,512]{1,0:T(8,128)(2,1)S(1)}, bf16[512,512]{1,0:T(8,128)(2,1)S(1)}) custom-call(f32[2,2,128,256]{3,2,1,0:T(8,128)S(1)} %copy-done.1, f32[3,2,128,256]{3,2,1,0:T(8,128)S(1)} %collective-permute-done.y_ref, f32[3,2,128,256]{3,2,1,0:T(8,128)} %collective-permute-done.2.z_ref, ...), custom_call_target="tpu_custom_call" | custom-call | bytes 2621440 | tf_op jit(solution)/shard_map/pallas_call | solution.py:340
  70.7 0.0 collective-permute-done.4.refs_1_
  70.7 1.4 %collective-permute-done.6.refs_3_ = f32[128,256]{1,0:T(8,128)S(1)} collective-permute-done((f32[128,256]{1,0:T(8,128)S(1)}, f32[128,256]{1,0:T(8,128)S(1)}, u32[]{:S(2)}, u32[]{:S(2)}) %collective-permute-start.6) | collective-permute-done | bytes 131104 | tf_op jit(solution)/shard_map/ppermute | solution.py:278
  72.1 0.3 shard_map.91
  72.4 0.1 collective-permute-start.7
  72.5 0.8 shard_map.89
  73.3 1.4 %collective-permute-start.10 = (f32[128,512]{1,0:T(8,128)S(1)}, f32[128,512]{1,0:T(8,128)S(1)}, u32[]{:S(2)}, u32[]{:S(2)}) collective-permute-start(f32[128,512]{1,0:T(8,128)S(1)} %get-tuple-element.35.refs_0_), channel_id=1, source_target_pairs={{0,4},{1,5},{2,6},{3,7},{4,0},{5,1},{6,2},{7,3},{8,12},{9,13},{10,... | collective-permute-start | bytes 786440 | tf_op jit(solution)/shard_map/ppermute | solution.py:278
  74.7 0.6 collective-permute-start.9
  75.3 0.0 collective-permute-done.7.refs_4_
  75.3 0.3 shard_map.92
  75.6 6.4 %collective-permute-done.10.x_ref.refs_2_ = f32[128,512]{1,0:T(8,128)S(1)} collective-permute-done((f32[128,512]{1,0:T(8,128)S(1)}, f32[128,512]{1,0:T(8,128)S(1)}, u32[]{:S(2)}, u32[]{:S(2)}) %collective-permute-start.10) | collective-permute-done | bytes 262176 | tf_op jit(solution)/shard_map/ppermute | solution.py:278
  82.0 1.3 collective-permute-start.11
  83.3 0.7 collective-permute-start.8
  84.0 6.0 %collective-permute-done.11.refs_3_ = f32[128,512]{1,0:T(8,128)S(1)} collective-permute-done((f32[128,512]{1,0:T(8,128)S(1)}, f32[128,512]{1,0:T(8,128)S(1)}, u32[]{:S(2)}, u32[]{:S(2)}) %collective-permute-start.11) | collective-permute-done | bytes 262176 | tf_op jit(solution)/shard_map/ppermute | solution.py:278
  90.0 7.4 %collective-permute-done.8.refs_4_.refs_1_ = f32[256,256]{1,0:T(8,128)S(1)} collective-permute-done((f32[256,256]{1,0:T(8,128)S(1)}, f32[256,256]{1,0:T(8,128)S(1)}, u32[]{:S(2)}, u32[]{:S(2)}) %collective-permute-start.8) | collective-permute-done | bytes 262176 | tf_op jit(solution)/shard_map/ppermute | solution.py:278
  97.4 0.4 shard_map.94
  97.9 0.1 collective-permute-start.12
  98.0 2.6 %collective-permute-done.12.refs_4_ = f32[512,512]{1,0:T(8,128)S(1)} collective-permute-done((f32[512,512]{1,0:T(8,128)S(1)}, f32[512,512]{1,0:T(8,128)S(1)}, u32[]{:S(2)}, u32[]{:S(2)}) %collective-permute-start.12) | collective-permute-done | bytes 1048608 | tf_op jit(solution)/shard_map/ppermute | solution.py:278
  100.6 0.4 shard_map.95
  101.0 0.1 collective-permute-start.13
  101.2 3.1 %convolution_convert_fusion = bf16[128,4096]{1,0:T(8,128)(2,1)} fusion(bf16[128,768]{1,0:T(8,128)(2,1)S(1)} %get-tuple-element.28, bf16[4096,768]{1,0:T(8,128)(2,1)S(1)} %bitcast.3), kind=kOutput, calls=%fused_computation | convolution fusion | flops 805830656 | bytes 7536640 | tf_op jit(solution)/shard_map/dot_general | solution.py:348
  104.3 21.9 %collective-permute-done.13.refs_3_ = f32[256,512]{1,0:T(8,128)S(1)} collective-permute-done((f32[256,512]{1,0:T(8,128)S(1)}, f32[256,512]{1,0:T(8,128)S(1)}, u32[]{:S(2)}, u32[]{:S(2)}) %collective-permute-start.13) | collective-permute-done | bytes 524320 | tf_op jit(solution)/shard_map/ppermute | solution.py:278
  126.2 1.0 shard_map.96
  (15 shorter events, 0.0 us)
Async XLA Ops:
  0.6 39.4 %copy-start = (bf16[3648,256]{1,0:T(8,128)(2,1)S(1)}, bf16[3648,256]{1,0:T(8,128)(2,1)}, u32[]{:S(2)}) copy-start(bf16[3648,256]{1,0:T(8,128)(2,1)} %constant.4.clone.table_ref) | copy-start | bytes 5603332
  4.2 22.2 %collective-permute-start = (f32[3,2,128,256]{3,2,1,0:T(8,128)}, f32[3,2,128,256]{3,2,1,0:T(8,128)S(1)}, u32[]{:S(2)}, u32[]{:S(2)}) collective-permute-start(f32[3,2,128,256]{3,2,1,0:T(8,128)} %get-tuple-element.22), channel_id=1, source_target_pairs={{0,2},{1,3},{2,0},{3,1},{4,6},{5,7},{6,4},{7,5},{8,10},{9,11},{10,... | collective-permute-start | bytes 2359304 | tf_op jit(solution)/shard_map/ppermute | solution.py:278
  7.2 24.5 %collective-permute-start.2 = (f32[3,2,128,256]{3,2,1,0:T(8,128)}, f32[3,2,128,256]{3,2,1,0:T(8,128)}, u32[]{:S(2)}, u32[]{:S(2)}) collective-permute-start(f32[3,2,128,256]{3,2,1,0:T(8,128)} %get-tuple-element.23), channel_id=1, source_target_pairs={{0,4},{1,5},{2,6},{3,7},{4,0},{5,1},{6,2},{7,3},{8,12},{9,13},{10,... | collective-permute-start | bytes 2359304 | tf_op jit(solution)/shard_map/ppermute | solution.py:278
  14.4 58.1 %copy-start.3 = (f32[256,128]{1,0:T(8,128)S(1)}, f32[256,128]{1,0:T(8,128)}, u32[]{:S(2)}) copy-start(f32[256,128]{1,0:T(8,128)} %get-tuple-element.24.key_ref) | copy-start | bytes 393220
  14.4 21.8 %all-to-all-start = ((f32[16,3,16,128]{3,2,1,0:T(8,128)}), f32[16,3,16,128]{3,2,1,0:T(8,128)S(1)}, u32[]{:S(2)}, u32[]{:S(2)}) async-start(f32[16,3,16,128]{3,2,1,0:T(8,128)} %get-tuple-element.21), calls=%async_computation | async-start | bytes 786432 | tf_op jit(solution)/shard_map/all_to_all | solution.py:313
  27.2 11.1 %collective-permute-start.1 = (f32[1,2,128,256]{3,2,1,0:T(8,128)}, f32[1,2,128,256]{3,2,1,0:T(8,128)S(1)}, u32[]{:S(2)}, u32[]{:S(2)}) collective-permute-start(f32[1,2,128,256]{3,2,1,0:T(8,128)} %slice.8), channel_id=1, source_target_pairs={{0,4},{1,5},{2,6},{3,7},{4,0},{5,1},{6,2},{7,3},{8,12},{9,13},{10,... | collective-permute-start | bytes 786440 | tf_op jit(solution)/shard_map/ppermute | solution.py:278
  33.3 6.7 %collective-permute-start.3 = (f32[1,2,128,256]{3,2,1,0:T(8,128)}, f32[1,2,128,256]{3,2,1,0:T(8,128)}, u32[]{:S(2)}, u32[]{:S(2)}) collective-permute-start(f32[1,2,128,256]{3,2,1,0:T(8,128)} %slice.9), channel_id=1, source_target_pairs={{0,2},{1,3},{2,0},{3,1},{4,6},{5,7},{6,4},{7,5},{8,10},{9,11},{10,... | collective-permute-start | bytes 786440 | tf_op jit(solution)/shard_map/ppermute | solution.py:278
  40.0 1.0 copy-start.2
  41.0 31.5 %copy-start.4 = (f32[256,128]{1,0:T(8,128)S(1)}, f32[256,128]{1,0:T(8,128)}, u32[]{:S(2)}) copy-start(f32[256,128]{1,0:T(8,128)} %get-tuple-element.25.value_ref) | copy-start | bytes 393220
  60.6 0.9 copy-start.5
  61.6 5.6 %collective-permute-start.5 = (f32[128,256]{1,0:T(8,128)S(1)}, f32[128,256]{1,0:T(8,128)S(1)}, u32[]{:S(2)}, u32[]{:S(2)}) collective-permute-start(f32[128,256]{1,0:T(8,128)S(1)} %get-tuple-element.31.refs_0_), channel_id=1, source_target_pairs={{0,4},{1,5},{2,6},{3,7},{4,0},{5,1},{6,2},{7,3},{8,12},{9,13},{10,... | collective-permute-start | bytes 393224 | tf_op jit(solution)/shard_map/ppermute | solution.py:278
  62.4 8.4 %collective-permute-start.4 = (f32[128,256]{1,0:T(8,128)S(1)}, f32[128,256]{1,0:T(8,128)S(1)}, u32[]{:S(2)}, u32[]{:S(2)}) collective-permute-start(f32[128,256]{1,0:T(8,128)S(1)} %get-tuple-element.31.refs_0_), channel_id=1, source_target_pairs={{0,2},{1,3},{2,0},{3,1},{4,6},{5,7},{6,4},{7,5},{8,10},{9,11},{10,... | collective-permute-start | bytes 393224 | tf_op jit(solution)/shard_map/ppermute | solution.py:278
  67.2 5.0 %collective-permute-start.6 = (f32[128,256]{1,0:T(8,128)S(1)}, f32[128,256]{1,0:T(8,128)S(1)}, u32[]{:S(2)}, u32[]{:S(2)}) collective-permute-start(f32[128,256]{1,0:T(8,128)S(1)} %collective-permute-done.5.refs_2_), channel_id=1, source_target_pairs={{0,2},{1,3},{2,0},{3,1},{4,6},{5,7},{6,4},{7,5},{8,10},{9,11},{10,... | collective-permute-start | bytes 393224 | tf_op jit(solution)/shard_map/ppermute | solution.py:278
  68.0 1.0 copy-start.1
  69.0 32.1 %slice-start = ((s8[6291456]{0:T(1024)(128)(4,1)}), s8[4194304]{0:T(1024)(128)(4,1)S(1)}, s32[]{:S(2)}) async-start(s8[6291456]{0:T(1024)(128)(4,1)} %bitcast.2), calls=%async_computation.2 | async-start | bytes 8388608
  72.4 2.9 %collective-permute-start.7 = (f32[512,256]{1,0:T(8,128)S(1)}, f32[512,256]{1,0:T(8,128)S(1)}, u32[]{:S(2)}, u32[]{:S(2)}) collective-permute-start(f32[512,256]{1,0:T(8,128)S(1)} %shard_map.91), channel_id=1, source_target_pairs={{0,1},{1,0},{2,3},{3,2},{4,5},{5,4},{6,7},{7,6},{8,9},{9,8},{10,11... | collective-permute-start | bytes 1572872 | tf_op jit(solution)/shard_map/ppermute | solution.py:278
  73.3 8.7 %collective-permute-start.10 = (f32[128,512]{1,0:T(8,128)S(1)}, f32[128,512]{1,0:T(8,128)S(1)}, u32[]{:S(2)}, u32[]{:S(2)}) collective-permute-start(f32[128,512]{1,0:T(8,128)S(1)} %get-tuple-element.35.refs_0_), channel_id=1, source_target_pairs={{0,4},{1,5},{2,6},{3,7},{4,0},{5,1},{6,2},{7,3},{8,12},{9,13},{10,... | collective-permute-start | bytes 786440 | tf_op jit(solution)/shard_map/ppermute | solution.py:278
  74.7 9.3 %collective-permute-start.9 = (f32[128,512]{1,0:T(8,128)S(1)}, f32[128,512]{1,0:T(8,128)S(1)}, u32[]{:S(2)}, u32[]{:S(2)}) collective-permute-start(f32[128,512]{1,0:T(8,128)S(1)} %get-tuple-element.35.refs_0_), channel_id=1, source_target_pairs={{0,2},{1,3},{2,0},{3,1},{4,6},{5,7},{6,4},{7,5},{8,10},{9,11},{10,... | collective-permute-start | bytes 786440 | tf_op jit(solution)/shard_map/ppermute | solution.py:278
  75.3 25.8 %slice-start.1 = ((s8[6291456]{0:T(1024)(128)(4,1)}), s8[2097152]{0:T(1024)(128)(4,1)S(1)}, s32[]{:S(2)}) async-start(s8[6291456]{0:T(1024)(128)(4,1)} %bitcast.2), calls=%async_computation.3 | async-start | bytes 4194304
  82.0 8.0 %collective-permute-start.11 = (f32[128,512]{1,0:T(8,128)S(1)}, f32[128,512]{1,0:T(8,128)S(1)}, u32[]{:S(2)}, u32[]{:S(2)}) collective-permute-start(f32[128,512]{1,0:T(8,128)S(1)} %shard_map.93), channel_id=1, source_target_pairs={{0,2},{1,3},{2,0},{3,1},{4,6},{5,7},{6,4},{7,5},{8,10},{9,11},{10,... | collective-permute-start | bytes 786440 | tf_op jit(solution)/shard_map/ppermute | solution.py:278
  83.3 14.1 %collective-permute-start.8 = (f32[256,256]{1,0:T(8,128)S(1)}, f32[256,256]{1,0:T(8,128)S(1)}, u32[]{:S(2)}, u32[]{:S(2)}) collective-permute-start(f32[256,256]{1,0:T(8,128)S(1)} %get-tuple-element.34), channel_id=1, source_target_pairs={{0,8},{1,9},{2,10},{3,11},{4,12},{5,13},{6,14},{7,15},{8,0},{9,1},... | collective-permute-start | bytes 786440 | tf_op jit(solution)/shard_map/ppermute | solution.py:278
  97.9 2.7 %collective-permute-start.12 = (f32[512,512]{1,0:T(8,128)S(1)}, f32[512,512]{1,0:T(8,128)S(1)}, u32[]{:S(2)}, u32[]{:S(2)}) collective-permute-start(f32[512,512]{1,0:T(8,128)S(1)} %shard_map.94), channel_id=1, source_target_pairs={{0,1},{1,0},{2,3},{3,2},{4,5},{5,4},{6,7},{7,6},{8,9},{9,8},{10,11... | collective-permute-start | bytes 3145736 | tf_op jit(solution)/shard_map/ppermute | solution.py:278
  101.0 25.2 %collective-permute-start.13 = (f32[256,512]{1,0:T(8,128)S(1)}, f32[256,512]{1,0:T(8,128)S(1)}, u32[]{:S(2)}, u32[]{:S(2)}) collective-permute-start(f32[256,512]{1,0:T(8,128)S(1)} %get-tuple-element.37), channel_id=1, source_target_pairs={{0,8},{1,9},{2,10},{3,11},{4,12},{5,13},{6,14},{7,15},{8,0},{9,1},... | collective-permute-start | bytes 1572872 | tf_op jit(solution)/shard_map/ppermute | solution.py:278

commit v2 on v1

--- a/solution.py
+++ b/solution.py
@@ -183,64 +183,65 @@
             y_ref[p, s] = result[p * width : (p + 1) * width, s * rows : (s + 1) * rows]
 
 
-def gate_first_kernel(y_ref, go_ref, gp_ref, sent_ref, flat):
-    count, _, width, _ = y_ref.shape
-    for owner in range(count):
-        flat[owner * width : (owner + 1) * width] = y_ref[owner, 0]
-    rounded = (go_ref[...] * flat[...]).T.astype(jnp.bfloat16)
-    gp_ref[...] = rounded
-    sent_ref[...] = rounded.astype(jnp.float32)
-
-
-def gate_rest_kernel(scaling, y_ref, key_ref, value_ref, first_ref, *refs):
-    gp_ref, sent_ref, taps_ref, flat = refs
+def gate_kernel(scaling, y_ref, go_ref, value_ref, key_ref, *refs):
+    gp_ref, first_ref, rest_ref, taps_ref, flat = refs[-5:]
     count, _, width, _ = y_ref.shape
     channels = count * width
-    for s in range(2):
+    for s in range(3):
         for owner in range(count):
-            flat[s, owner * width : (owner + 1) * width] = y_ref[owner, s + 1]
-    gp_ref[:, :channels] = first_ref[...]
-    for index, factor_ref in enumerate((value_ref, key_ref)):
-        rounded = (factor_ref[...] * flat[0]).T.astype(jnp.bfloat16)
-        gp_ref[:, (index + 1) * channels : (index + 2) * channels] = rounded
-        sent_ref[:, index * channels : (index + 1) * channels] = rounded.astype(jnp.float32)
-    taps_ref[...] = flat[1].T * scaling
-
-
-def relay_kernel(x_ref, *refs):
-    refs[-1][...] = x_ref[...]
-
-
-def turn_kernel(own_ref, y_ref, z_ref, corner_own_ref, corner_other_ref, *out_refs):
-    _, far, rows, part = own_ref.shape
-    sources = (
-        ((own_ref, 0), (y_ref, 0), (z_ref, 2), (corner_own_ref, 0)),
-        ((own_ref, 1), (y_ref, 2), (z_ref, 0), (corner_other_ref, 0)),
-    )
-    for out_ref, chips in zip(out_refs, sources):
-        for which, (x_ref, slot) in enumerate(chips):
-            for f in range(far):
-                out_ref[f * part : (f + 1) * part, which * rows : (which + 1) * rows] = (
-                    x_ref[slot, f].T.astype(jnp.bfloat16)
-                )
+            flat[s, owner * width : (owner + 1) * width] = y_ref[owner, s]
+    for index, factor_ref in enumerate((go_ref, value_ref, key_ref)):
+        rounded = (factor_ref[...] * flat[min(index, 1)]).T.astype(jnp.bfloat16)
+        gp_ref[:, index * channels : (index + 1) * channels] = rounded
+        if index == 0:
+            first_ref[...] = rounded.astype(jnp.float32)
+        else:
+            span = slice((index - 1) * channels, index * channels)
+            rest_ref[:, span] = rounded.astype(jnp.float32)
+    taps_ref[...] = flat[2].T * scaling
+
+
+def turn_blocks(sources, out_ref):
+    for which, (x_ref, slot) in enumerate(sources):
+        _, far, rows, part = x_ref.shape
+        for f in range(far):
+            out_ref[f * part : (f + 1) * part, which * rows : (which + 1) * rows] = x_ref[
+                slot, f
+            ].T.astype(jnp.bfloat16)
+
+
+def turn_kernel(own_ref, y_ref, z_ref, out_own_ref, out_other_ref):
+    turn_blocks(((own_ref, 0), (y_ref, 0), (z_ref, 2)), out_own_ref)
+    turn_blocks(((own_ref, 1), (y_ref, 2), (z_ref, 0)), out_other_ref)
+
+
+def corner_kernel(corner_own_ref, corner_other_ref, out_own_ref, out_other_ref):
+    turn_blocks(((corner_own_ref, 0),), out_own_ref)
+    turn_blocks(((corner_other_ref, 0),), out_other_ref)
+
+
+def joined_columns(x_ref, corner_ref, span):
+    return jnp.concatenate([x_ref[span], corner_ref[span]], axis=1)
 
 
 def joined(gp_refs):
     return jnp.concatenate([gp_ref[...].astype(jnp.bfloat16) for gp_ref in gp_refs], axis=0)
 
 
-def other_kernel(x_ref, *refs):
+def other_kernel(x_ref, corner_ref, *refs):
     gp_refs, out_ref = refs[:SIDE], refs[-1]
-    out_ref[...] = jnp.dot(x_ref[...], joined(gp_refs), preferred_element_type=jnp.float32)
-
-
-def own_kernel(x_ref, *refs):
+    columns = joined_columns(x_ref, corner_ref, slice(None))
+    out_ref[...] = jnp.dot(columns, joined(gp_refs), preferred_element_type=jnp.float32)
+
+
+def own_kernel(x_ref, corner_ref, *refs):
     gp_refs, add_ref, out_refs = refs[:SIDE], refs[SIDE], refs[SIDE + 1 :]
     gp = joined(gp_refs)
     part = out_refs[0].shape[0]
     for which, out_ref in enumerate(out_refs):
         span = slice(which * part, (which + 1) * part)
-        product = jnp.dot(x_ref[span], gp, preferred_element_type=jnp.float32)
+        columns = joined_columns(x_ref, corner_ref, span)
+        product = jnp.dot(columns, gp, preferred_element_type=jnp.float32)
         out_ref[...] = product + add_ref[span]
 
 
@@ -286,7 +287,14 @@
     )(inputs)
     from_y, from_z = exchange(to_y, 2), exchange(to_z, 4)
     corners = exchange(from_y[1:2], 4), exchange(from_z[1:2], 2)
-    held = (own, from_y, from_z) + corners
+    turned = pl.pallas_call(
+        turn_kernel,
+        out_shape=[shaped(far * part, (SIDE - 1) * rows, dtype=bf16)] * 2,
+        compiler_params=params,
+        cost_estimate=pl.CostEstimate(
+            flops=0, bytes_accessed=200 * SIDE * far * rows * part, transcendentals=0
+        ),
+    )(own, from_y, from_z)
     signals, gate_out, key, value = pl.pallas_call(
         functools.partial(project_kernel, scaling),
         grid=(steps,),
@@ -319,48 +327,32 @@
         out_shape=shaped(blocks, 3, width, rows),
         scratch_shapes=[pltpu.VMEM((blocks * width, 3 * rows), f32)],
         compiler_params=params,
-    )(signals, jnp.asarray(table), jnp.asarray(turn), *corners)
+    )(signals, jnp.asarray(table), jnp.asarray(turn), *turned)
     results = lax.all_to_all(results, "seq", split_axis=0, concat_axis=0, tiled=True)
-    first, sent_first = pl.pallas_call(
-        gate_first_kernel,
-        out_shape=[shaped(rows, channels, dtype=bf16), shaped(rows, channels)],
-        scratch_shapes=[pltpu.VMEM((channels, rows), f32)],
-        compiler_params=params,
-    )(results, gate_out)
-    grad_proj, sent_rest, grad_taps = pl.pallas_call(
-        functools.partial(gate_rest_kernel, scaling),
+    grad_proj, sent_first, sent_rest, grad_taps = pl.pallas_call(
+        functools.partial(gate_kernel, scaling),
+        in_specs=[inside] * 4 + [anywhere] * 2,
         out_shape=[
             shaped(rows, columns, dtype=bf16),
+            shaped(rows, channels),
             shaped(rows, 2 * channels),
             shaped(rows, channels),
         ],
-        scratch_shapes=[pltpu.VMEM((2, channels, rows), f32)],
-        compiler_params=params,
-    )(results, key, value, first)
-    turned = pl.pallas_call(
-        turn_kernel,
-        out_shape=[shaped(far * part, SIDE * rows, dtype=bf16)] * 2,
-        compiler_params=params,
-        cost_estimate=pl.CostEstimate(
-            flops=0, bytes_accessed=10 * SIDE * far * rows * part, transcendentals=0
-        ),
-    )(*held)
+        scratch_shapes=[pltpu.VMEM((3, channels, rows), f32)],
+        compiler_params=params,
+    )(results, gate_out, value, key, *corners)
+    turned_corners = pl.pallas_call(
+        corner_kernel,
+        out_shape=[shaped(far * part, rows, dtype=bf16)] * 2,
+        compiler_params=params,
+    )(*corners)
     grad_inputs = lax.dot_general(
         grad_proj, in_weight, (((1,), (1,)), ((), ())), preferred_element_type=f32
     ).astype(bf16)
     terms = []
     for block in (sent_first, sent_rest):
         cols = block.shape[1]
-        from_far = exchange(block, 4)
-        relayed = from_far
-        if terms:
-            relayed = pl.pallas_call(
-                relay_kernel,
-                in_specs=[inside, anywhere],
-                out_shape=shaped(rows, cols),
-                compiler_params=params,
-            )(from_far, terms[0])
-        gathered = [block, exchange(block, 2), from_far, exchange(relayed, 2)]
+        gathered = [block] + [exchange(block, 2 * k) for k in range(1, SIDE)]
         cost = pl.CostEstimate(
             flops=2 * far * part * SIDE * rows * cols,
             bytes_accessed=4 * far * part * cols,
@@ -368,17 +360,17 @@
         )
         other = pl.pallas_call(
             other_kernel,
-            in_specs=[inside] * (1 + SIDE) + [anywhere] * len(terms[1:]),
+            in_specs=[inside] * (2 + SIDE) + [anywhere] * len(terms[1:]),
             out_shape=shaped(far * part, cols),
             compiler_params=params,
             cost_estimate=cost,
-        )(turned[1], *gathered, *terms[1:])
+        )(turned[1], turned_corners[1], *gathered, *terms[1:])
         kept, *leaving = pl.pallas_call(
             own_kernel,
             out_shape=[shaped(part, cols)] * far,
             compiler_params=params,
             cost_estimate=cost,
-        )(turned[0], *gathered, exchange(other, 1))
+        )(turned[0], turned_corners[0], *gathered, exchange(other, 1))
         terms += [kept] + [exchange(v, 2 * SIDE * (k + 1)) for k, v in enumerate(leaving)]
     grad_weight = pl.pallas_call(
         functools.partial(sum_kernel, scaling, 2),

time: 128 us -> 123 us (0.961)
  blocking collectives: 17 us -> 0 us
  starting transfers between devices: 17.2 us -> 28.5 us
  waiting for transfers between devices: 67 us -> 63.4 us
  matrix products: 3.11 us -> 5.89 us
  local copies, waits for them, and re-layouts: 5.31 us -> 6.81 us
    all_to_all x1 -> x0, blocking collectives: 17 us -> none  [per_device(): lax.all_to_all(results, 'seq', split_axis=0, concat_axis=0, tiled=True)]
    all_to_all x0 -> x1, starting transfers between devices: none -> 5.9 us  [per_device(): lax.all_to_all(results, 'seq', split_axis=0, concat_axis=0, tiled=True)]
    ppermute x14, starting transfers between devices: 13.1 us -> 18.5 us  [exchange(): return lax.ppermute(value, 'seq', [(i, i ^ flip) for i in range(blocks)])]
    all_to_all x1, waiting for transfers between devices: 2.84 us -> 0.04 us  [per_device(): lax.all_to_all(signals, 'seq', split_axis=0, concat_axis=0, tiled=True)]
    dot_general x1, matrix products: 3.11 us -> 5.89 us  [per_device(): lax.dot_general(grad_proj, in_weight, (((1,), (1,)), ((), ())), preferred...]
    unnamed x16, local copies, waits for them, and re-layouts: 2.92 us -> 4.87 us
    pallas_call x6 -> x5, Pallas kernels: 3.32 us -> 3.09 us  [the longest x1 1.4 us: per_device(): pl.pallas_call(turn_kernel, out_shape=[shaped(far * part, (SIDE - 1) * ro...]
  transfers between devices with their start and end apart: 15 -> 16, of which waited for: 12 -> 10; matrix products, arithmetic and copies ran while one was open for 4% -> 6% of each run, Pallas kernels for 7% -> 6%
where the time goes in v2:
time: 123 us
  waiting for transfers between devices  63.4 us (52%)
  starting transfers between devices  28.5 us (23%)
  Pallas kernels  17.4 us (14%)
  local copies, waits for them, and re-layouts  6.81 us (6%)
  matrix products  5.89 us (5%)
    ppermute x14, waiting for transfers between devices, exchange(): return lax.ppermute(value, 'seq', [(i, i ^ flip) for i in range(blocks)])  63.3 us
    ppermute x14, starting transfers between devices, exchange(): return lax.ppermute(value, 'seq', [(i, i ^ flip) for i in range(blocks)])  18.5 us
    all_to_all x1, starting transfers between devices, per_device(): lax.all_to_all(results, 'seq', split_axis=0, concat_axis=0, tiled=True)  5.9 us
    dot_general x1, matrix products, per_device(): lax.dot_general(grad_proj, in_weight, (((1,), (1,)), ((), ())), preferred...  5.89 us
    pallas_call x1, Pallas kernels, per_device(): pl.pallas_call(functools.partial(project_kernel, scaling), grid=(steps,),...  5.63 us
    unnamed x16, local copies, waits for them, and re-layouts  4.87 us
    all_to_all x1, starting transfers between devices, per_device(): lax.all_to_all(signals, 'seq', split_axis=0, concat_axis=0, tiled=True)  4.1 us
    pallas_call x1, Pallas kernels, per_device(): pl.pallas_call(layout_kernel, out_shape=[shaped(2, far, rows, part)] + [s...  3.61 us
  transfers between devices with their start and end apart: 16, of which 10 were waited for; matrix products, arithmetic and copies ran while one was open for 6% of the time, Pallas kernels for 6%

profile of v2, /device:TPU:0, one launch (start us, length us, event | category | flops | bytes accessed | tf_op | source)
XLA Modules:
  0.0 122.7 jit_solution(898007733561024312)
XLA Ops:
  0.6 0.0 copy-start
  0.6 0.0 copy-start.4
  0.7 3.6 %shard_map.86 = (f32[2,2,128,256]{3,2,1,0:T(8,128)}, f32[3,2,128,256]{3,2,1,0:T(8,128)}, f32[3,2,128,256]{3,2,1,0:T(8,128)}) custom-call(bf16[128,4096]{1,0:T(8,128)(2,1)} %x_ref.3), custom_call_target="tpu_custom_call" | custom-call | tf_op jit(solution)/shard_map/pallas_call | solution.py:283
  4.3 3.0 %collective-permute-start = (f32[3,2,128,256]{3,2,1,0:T(8,128)}, f32[3,2,128,256]{3,2,1,0:T(8,128)}, u32[]{:S(2)}, u32[]{:S(2)}) collective-permute-start(f32[3,2,128,256]{3,2,1,0:T(8,128)} %get-tuple-element.24), channel_id=1, source_target_pairs={{0,2},{1,3},{2,0},{3,1},{4,6},{5,7},{6,4},{7,5},{8,10},{9,11},{10,... | collective-permute-start | bytes 2359304 | tf_op jit(solution)/shard_map/ppermute | solution.py:279
  7.2 1.6 %collective-permute-start.1 = (f32[3,2,128,256]{3,2,1,0:T(8,128)}, f32[3,2,128,256]{3,2,1,0:T(8,128)S(1)}, u32[]{:S(2)}, u32[]{:S(2)}) collective-permute-start(f32[3,2,128,256]{3,2,1,0:T(8,128)} %get-tuple-element.25), channel_id=1, source_target_pairs={{0,4},{1,5},{2,6},{3,7},{4,0},{5,1},{6,2},{7,3},{8,12},{9,13},{10,... | collective-permute-start | bytes 2359304 | tf_op jit(solution)/shard_map/ppermute | solution.py:279
  8.8 5.6 %shard_map.85 = (f32[16,3,16,128]{3,2,1,0:T(8,128)}, f32[256,128]{1,0:T(8,128)}, f32[256,128]{1,0:T(8,128)}, f32[256,128]{1,0:T(8,128)}) custom-call(bf16[128,4096]{1,0:T(8,128)(2,1)} %x_ref.3, bf16[4096,768]{1,0:T(8,128)(2,1)} %w_ref.1, f32[128,256]{1,0:T(8,128)} %taps_ref.1, bf16[128,256]{1,0:T(8,128)(2,1)} %go_ref.1), custom_call_target="tpu_custom_call" | custom-call | flops 805306368 | bytes 7340032 | tf_op jit(solution)/shard_map/pallas_call | solution.py:298
  14.4 4.1 %all-to-all-start = ((f32[16,3,16,128]{3,2,1,0:T(8,128)}), f32[16,3,16,128]{3,2,1,0:T(8,128)S(1)}, u32[]{:S(2)}, u32[]{:S(2)}) async-start(f32[16,3,16,128]{3,2,1,0:T(8,128)} %get-tuple-element.22), calls=%async_computation | async-start | bytes 786432 | tf_op jit(solution)/shard_map/all_to_all | solution.py:321
  18.5 8.1 %collective-permute-done.y_ref = f32[3,2,128,256]{3,2,1,0:T(8,128)} collective-permute-done((f32[3,2,128,256]{3,2,1,0:T(8,128)}, f32[3,2,128,256]{3,2,1,0:T(8,128)}, u32[]{:S(2)}, u32[]{:S(2)}) %collective-permute-start) | collective-permute-done | bytes 786464 | tf_op jit(solution)/shard_map/ppermute | solution.py:279
  26.6 3.6 %collective-permute-done.1.z_ref = f32[3,2,128,256]{3,2,1,0:T(8,128)S(1)} collective-permute-done((f32[3,2,128,256]{3,2,1,0:T(8,128)}, f32[3,2,128,256]{3,2,1,0:T(8,128)S(1)}, u32[]{:S(2)}, u32[]{:S(2)}) %collective-permute-start.1) | collective-permute-done | bytes 786464 | tf_op jit(solution)/shard_map/ppermute | solution.py:279
  30.2 0.9 copy-done.1
  31.1 1.1 copy-done.2
  32.2 1.0 copy-done.3
  33.3 1.4 %shard_map.87 = (bf16[512,384]{1,0:T(8,128)(2,1)S(1)}, bf16[512,384]{1,0:T(8,128)(2,1)S(1)}) custom-call(f32[2,2,128,256]{3,2,1,0:T(8,128)S(1)} %copy-done.3, f32[3,2,128,256]{3,2,1,0:T(8,128)} %collective-permute-done.y_ref, f32[3,2,128,256]{3,2,1,0:T(8,128)S(1)} %copy-done.2), custom_call_target="tpu_custom_call" | custom-call | bytes 52428800 | tf_op jit(solution)/shard_map/pallas_call | solution.py:290
  34.7 0.0 all-to-all-done.x_ref
  34.7 3.3 %shard_map.88 = f32[16,3,16,128]{3,2,1,0:T(8,128)} custom-call(f32[16,3,16,128]{3,2,1,0:T(8,128)S(1)} %all-to-all-done.x_ref, bf16[3648,256]{1,0:T(8,128)(2,1)S(1)} %copy-done, f32[272,256]{1,0:T(8,128)S(1)} %copy-done.4, bf16[512,384]{1,0:T(8,128)(2,1)S(1)} %get-tuple-element.26.refs_0_.x_ref, bf16[512,384]{1,0:T(8,128)(2,1)S(1)} %get-tuple-element.27.refs_1_.x_ref), custom_call_target="tpu_custom_call" | custom-call | tf_op jit(solution)/shard_map/pallas_call | solution.py:324
  38.1 5.9 %all-to-all-start.1 = ((f32[16,3,16,128]{3,2,1,0:T(8,128)}), f32[16,3,16,128]{3,2,1,0:T(8,128)S(1)}, u32[]{:S(2)}, u32[]{:S(2)}) async-start(f32[16,3,16,128]{3,2,1,0:T(8,128)} %shard_map.88), calls=%async_computation.1 | async-start | bytes 786432 | tf_op jit(solution)/shard_map/all_to_all | solution.py:331
  44.0 1.0 slice.8
  44.9 2.0 %collective-permute-start.2 = (f32[1,2,128,256]{3,2,1,0:T(8,128)S(1)}, f32[1,2,128,256]{3,2,1,0:T(8,128)S(1)}, u32[]{:S(2)}, u32[]{:S(2)}) collective-permute-start(f32[1,2,128,256]{3,2,1,0:T(8,128)S(1)} %slice.8), channel_id=1, source_target_pairs={{0,4},{1,5},{2,6},{3,7},{4,0},{5,1},{6,2},{7,3},{8,12},{9,13},{10,... | collective-permute-start | bytes 786440 | tf_op jit(solution)/shard_map/ppermute | solution.py:279
  46.9 1.0 slice.9
  47.9 1.5 %collective-permute-start.3 = (f32[1,2,128,256]{3,2,1,0:T(8,128)S(1)}, f32[1,2,128,256]{3,2,1,0:T(8,128)S(1)}, u32[]{:S(2)}, u32[]{:S(2)}) collective-permute-start(f32[1,2,128,256]{3,2,1,0:T(8,128)S(1)} %slice.9), channel_id=1, source_target_pairs={{0,2},{1,3},{2,0},{3,1},{4,6},{5,7},{6,4},{7,5},{8,10},{9,11},{10,... | collective-permute-start | bytes 786440 | tf_op jit(solution)/shard_map/ppermute | solution.py:279
  49.4 9.6 %collective-permute-done.2.refs_0_.corner_own_ref = f32[1,2,128,256]{3,2,1,0:T(8,128)S(1)} collective-permute-done((f32[1,2,128,256]{3,2,1,0:T(8,128)S(1)}, f32[1,2,128,256]{3,2,1,0:T(8,128)S(1)}, u32[]{:S(2)}, u32[]{:S(2)}) %collective-permute-start.2) | collective-permute-done | bytes 262176 | tf_op jit(solution)/shard_map/ppermute | solution.py:279
  59.1 0.9 copy-done.6
  60.0 0.9 copy-done.7
  60.9 0.8 shard_map.89
  61.7 1.5 %collective-permute-start.4 = (f32[128,256]{1,0:T(8,128)S(1)}, f32[128,256]{1,0:T(8,128)S(1)}, u32[]{:S(2)}, u32[]{:S(2)}) collective-permute-start(f32[128,256]{1,0:T(8,128)S(1)} %get-tuple-element.33.refs_0_), channel_id=1, source_target_pairs={{0,2},{1,3},{2,0},{3,1},{4,6},{5,7},{6,4},{7,5},{8,10},{9,11},{10,... | collective-permute-start | bytes 393224 | tf_op jit(solution)/shard_map/ppermute | solution.py:279
  63.2 0.6 collective-permute-start.5
  63.7 1.5 %collective-permute-start.6 = (f32[128,256]{1,0:T(8,128)S(1)}, f32[128,256]{1,0:T(8,128)S(1)}, u32[]{:S(2)}, u32[]{:S(2)}) collective-permute-start(f32[128,256]{1,0:T(8,128)S(1)} %get-tuple-element.33.refs_0_), channel_id=1, source_target_pairs={{0,6},{1,7},{2,4},{3,5},{4,2},{5,3},{6,0},{7,1},{8,14},{9,15},{10,... | collective-permute-start | bytes 393224 | tf_op jit(solution)/shard_map/ppermute | solution.py:279
  65.2 0.1 shard_map.90
  65.3 1.9 %collective-permute-done.4.refs_1_ = f32[128,256]{1,0:T(8,128)S(1)} collective-permute-done((f32[128,256]{1,0:T(8,128)S(1)}, f32[128,256]{1,0:T(8,128)S(1)}, u32[]{:S(2)}, u32[]{:S(2)}) %collective-permute-start.4) | collective-permute-done | bytes 131104 | tf_op jit(solution)/shard_map/ppermute | solution.py:279
  67.2 2.1 %collective-permute-done.5.refs_2_ = f32[128,256]{1,0:T(8,128)S(1)} collective-permute-done((f32[128,256]{1,0:T(8,128)S(1)}, f32[128,256]{1,0:T(8,128)S(1)}, u32[]{:S(2)}, u32[]{:S(2)}) %collective-permute-start.5) | collective-permute-done | bytes 131104 | tf_op jit(solution)/shard_map/ppermute | solution.py:279
  69.3 1.4 %collective-permute-done.6.refs_3_ = f32[128,256]{1,0:T(8,128)S(1)} collective-permute-done((f32[128,256]{1,0:T(8,128)S(1)}, f32[128,256]{1,0:T(8,128)S(1)}, u32[]{:S(2)}, u32[]{:S(2)}) %collective-permute-start.6) | collective-permute-done | bytes 131104 | tf_op jit(solution)/shard_map/ppermute | solution.py:279
  70.7 0.3 shard_map.91
  71.0 0.1 collective-permute-start.7
  71.1 0.8 collective-permute-start.10
  71.9 2.2 %collective-permute-start.11 = (f32[128,512]{1,0:T(8,128)S(1)}, f32[128,512]{1,0:T(8,128)S(1)}, u32[]{:S(2)}, u32[]{:S(2)}) collective-permute-start(f32[128,512]{1,0:T(8,128)S(1)} %get-tuple-element.37.refs_0_), channel_id=1, source_target_pairs={{0,6},{1,7},{2,4},{3,5},{4,2},{5,3},{6,0},{7,1},{8,14},{9,15},{10,... | collective-permute-start | bytes 786440 | tf_op jit(solution)/shard_map/ppermute | solution.py:279
  74.1 0.6 collective-permute-start.9
  74.7 0.3 shard_map.92
  75.0 2.5 %collective-permute-start.8 = (f32[256,256]{1,0:T(8,128)S(1)}, f32[256,256]{1,0:T(8,128)S(1)}, u32[]{:S(2)}, u32[]{:S(2)}) collective-permute-start(f32[256,256]{1,0:T(8,128)S(1)} %get-tuple-element.36), channel_id=1, source_target_pairs={{0,8},{1,9},{2,10},{3,11},{4,12},{5,13},{6,14},{7,15},{8,0},{9,1},... | collective-permute-start | bytes 786440 | tf_op jit(solution)/shard_map/ppermute | solution.py:279
  77.4 8.4 %collective-permute-done.10.refs_2_ = f32[128,512]{1,0:T(8,128)S(1)} collective-permute-done((f32[128,512]{1,0:T(8,128)S(1)}, f32[128,512]{1,0:T(8,128)S(1)}, u32[]{:S(2)}, u32[]{:S(2)}) %collective-permute-start.10) | collective-permute-done | bytes 262176 | tf_op jit(solution)/shard_map/ppermute | solution.py:279
  85.9 6.1 %collective-permute-done.11.refs_3_ = f32[128,512]{1,0:T(8,128)S(1)} collective-permute-done((f32[128,512]{1,0:T(8,128)S(1)}, f32[128,512]{1,0:T(8,128)S(1)}, u32[]{:S(2)}, u32[]{:S(2)}) %collective-permute-start.11) | collective-permute-done | bytes 262176 | tf_op jit(solution)/shard_map/ppermute | solution.py:279
  92.0 0.4 shard_map.93
  92.4 0.1 collective-permute-start.12
  92.5 2.6 %collective-permute-done.12.refs_4_ = f32[512,512]{1,0:T(8,128)S(1)} collective-permute-done((f32[512,512]{1,0:T(8,128)S(1)}, f32[512,512]{1,0:T(8,128)S(1)}, u32[]{:S(2)}, u32[]{:S(2)}) %collective-permute-start.12) | collective-permute-done | bytes 1048608 | tf_op jit(solution)/shard_map/ppermute | solution.py:279
  95.1 0.4 shard_map.94
  95.6 0.8 collective-permute-start.13
  96.4 5.9 %convolution_convert_fusion = bf16[128,4096]{1,0:T(8,128)(2,1)} fusion(bf16[128,768]{1,0:T(8,128)(2,1)S(1)} %get-tuple-element.31, bf16[4096,768]{1,0:T(8,128)(2,1)} %w_ref.1), kind=kOutput, calls=%fused_computation | convolution fusion | flops 805830656 | bytes 7536640 | tf_op jit(solution)/shard_map/dot_general | solution.py:349
  102.3 19.4 %collective-permute-done.13.refs_3_ = f32[256,512]{1,0:T(8,128)S(1)} collective-permute-done((f32[256,512]{1,0:T(8,128)S(1)}, f32[256,512]{1,0:T(8,128)S(1)}, u32[]{:S(2)}, u32[]{:S(2)}) %collective-permute-start.13) | collective-permute-done | bytes 524320 | tf_op jit(solution)/shard_map/ppermute | solution.py:279
  121.7 1.0 shard_map.95
  (14 shorter events, 0.0 us)
Async XLA Ops:
  0.6 34.1 %copy-start = (bf16[3648,256]{1,0:T(8,128)(2,1)S(1)}, bf16[3648,256]{1,0:T(8,128)(2,1)}, u32[]{:S(2)}) copy-start(bf16[3648,256]{1,0:T(8,128)(2,1)} %constant.4.clone.table_ref) | copy-start | bytes 5603332
  0.6 34.1 %copy-start.4 = (f32[272,256]{1,0:T(8,128)S(1)}, f32[272,256]{1,0:T(8,128)}, u32[]{:S(2)}) copy-start(f32[272,256]{1,0:T(8,128)} %constant.5.clone.turn_ref) | copy-start | bytes 835588
  4.3 22.3 %collective-permute-start = (f32[3,2,128,256]{3,2,1,0:T(8,128)}, f32[3,2,128,256]{3,2,1,0:T(8,128)}, u32[]{:S(2)}, u32[]{:S(2)}) collective-permute-start(f32[3,2,128,256]{3,2,1,0:T(8,128)} %get-tuple-element.24), channel_id=1, source_target_pairs={{0,2},{1,3},{2,0},{3,1},{4,6},{5,7},{6,4},{7,5},{8,10},{9,11},{10,... | collective-permute-start | bytes 2359304 | tf_op jit(solution)/shard_map/ppermute | solution.py:279
  7.2 23.0 %collective-permute-start.1 = (f32[3,2,128,256]{3,2,1,0:T(8,128)}, f32[3,2,128,256]{3,2,1,0:T(8,128)S(1)}, u32[]{:S(2)}, u32[]{:S(2)}) collective-permute-start(f32[3,2,128,256]{3,2,1,0:T(8,128)} %get-tuple-element.25), channel_id=1, source_target_pairs={{0,4},{1,5},{2,6},{3,7},{4,0},{5,1},{6,2},{7,3},{8,12},{9,13},{10,... | collective-permute-start | bytes 2359304 | tf_op jit(solution)/shard_map/ppermute | solution.py:279
  14.4 44.6 %copy-start.5 = (f32[256,128]{1,0:T(8,128)S(1)}, f32[256,128]{1,0:T(8,128)}, u32[]{:S(2)}) copy-start(f32[256,128]{1,0:T(8,128)} %get-tuple-element.28.go_ref) | copy-start | bytes 393220
  14.4 20.3 %all-to-all-start = ((f32[16,3,16,128]{3,2,1,0:T(8,128)}), f32[16,3,16,128]{3,2,1,0:T(8,128)S(1)}, u32[]{:S(2)}, u32[]{:S(2)}) async-start(f32[16,3,16,128]{3,2,1,0:T(8,128)} %get-tuple-element.22), calls=%async_computation | async-start | bytes 786432 | tf_op jit(solution)/shard_map/all_to_all | solution.py:321
  30.2 0.9 copy-start.1
  31.1 1.1 copy-start.2
  32.2 1.0 copy-start.3
  38.1 21.0 %all-to-all-start.1 = ((f32[16,3,16,128]{3,2,1,0:T(8,128)}), f32[16,3,16,128]{3,2,1,0:T(8,128)S(1)}, u32[]{:S(2)}, u32[]{:S(2)}) async-start(f32[16,3,16,128]{3,2,1,0:T(8,128)} %shard_map.88), calls=%async_computation.1 | async-start | bytes 786432 | tf_op jit(solution)/shard_map/all_to_all | solution.py:331
  44.9 14.1 %collective-permute-start.2 = (f32[1,2,128,256]{3,2,1,0:T(8,128)S(1)}, f32[1,2,128,256]{3,2,1,0:T(8,128)S(1)}, u32[]{:S(2)}, u32[]{:S(2)}) collective-permute-start(f32[1,2,128,256]{3,2,1,0:T(8,128)S(1)} %slice.8), channel_id=1, source_target_pairs={{0,4},{1,5},{2,6},{3,7},{4,0},{5,1},{6,2},{7,3},{8,12},{9,13},{10,... | collective-permute-start | bytes 786440 | tf_op jit(solution)/shard_map/ppermute | solution.py:279
  47.9 11.1 %collective-permute-start.3 = (f32[1,2,128,256]{3,2,1,0:T(8,128)S(1)}, f32[1,2,128,256]{3,2,1,0:T(8,128)S(1)}, u32[]{:S(2)}, u32[]{:S(2)}) collective-permute-start(f32[1,2,128,256]{3,2,1,0:T(8,128)S(1)} %slice.9), channel_id=1, source_target_pairs={{0,2},{1,3},{2,0},{3,1},{4,6},{5,7},{6,4},{7,5},{8,10},{9,11},{10,... | collective-permute-start | bytes 786440 | tf_op jit(solution)/shard_map/ppermute | solution.py:279
  59.0 0.9 copy-start.6
  60.0 0.9 copy-start.7
  61.7 5.5 %collective-permute-start.4 = (f32[128,256]{1,0:T(8,128)S(1)}, f32[128,256]{1,0:T(8,128)S(1)}, u32[]{:S(2)}, u32[]{:S(2)}) collective-permute-start(f32[128,256]{1,0:T(8,128)S(1)} %get-tuple-element.33.refs_0_), channel_id=1, source_target_pairs={{0,2},{1,3},{2,0},{3,1},{4,6},{5,7},{6,4},{7,5},{8,10},{9,11},{10,... | collective-permute-start | bytes 393224 | tf_op jit(solution)/shard_map/ppermute | solution.py:279
  63.2 6.2 %collective-permute-start.5 = (f32[128,256]{1,0:T(8,128)S(1)}, f32[128,256]{1,0:T(8,128)S(1)}, u32[]{:S(2)}, u32[]{:S(2)}) collective-permute-start(f32[128,256]{1,0:T(8,128)S(1)} %get-tuple-element.33.refs_0_), channel_id=1, source_target_pairs={{0,4},{1,5},{2,6},{3,7},{4,0},{5,1},{6,2},{7,3},{8,12},{9,13},{10,... | collective-permute-start | bytes 393224 | tf_op jit(solution)/shard_map/ppermute | solution.py:279
  63.7 7.0 %collective-permute-start.6 = (f32[128,256]{1,0:T(8,128)S(1)}, f32[128,256]{1,0:T(8,128)S(1)}, u32[]{:S(2)}, u32[]{:S(2)}) collective-permute-start(f32[128,256]{1,0:T(8,128)S(1)} %get-tuple-element.33.refs_0_), channel_id=1, source_target_pairs={{0,6},{1,7},{2,4},{3,5},{4,2},{5,3},{6,0},{7,1},{8,14},{9,15},{10,... | collective-permute-start | bytes 393224 | tf_op jit(solution)/shard_map/ppermute | solution.py:279
  71.0 3.6 %collective-permute-start.7 = (f32[512,256]{1,0:T(8,128)S(1)}, f32[512,256]{1,0:T(8,128)S(1)}, u32[]{:S(2)}, u32[]{:S(2)}) collective-permute-start(f32[512,256]{1,0:T(8,128)S(1)} %shard_map.91), channel_id=1, source_target_pairs={{0,1},{1,0},{2,3},{3,2},{4,5},{5,4},{6,7},{7,6},{8,9},{9,8},{10,11... | collective-permute-start | bytes 1572872 | tf_op jit(solution)/shard_map/ppermute | solution.py:279
  71.1 14.8 %collective-permute-start.10 = (f32[128,512]{1,0:T(8,128)S(1)}, f32[128,512]{1,0:T(8,128)S(1)}, u32[]{:S(2)}, u32[]{:S(2)}) collective-permute-start(f32[128,512]{1,0:T(8,128)S(1)} %get-tuple-element.37.refs_0_), channel_id=1, source_target_pairs={{0,4},{1,5},{2,6},{3,7},{4,0},{5,1},{6,2},{7,3},{8,12},{9,13},{10,... | collective-permute-start | bytes 786440 | tf_op jit(solution)/shard_map/ppermute | solution.py:279
  71.9 20.1 %collective-permute-start.11 = (f32[128,512]{1,0:T(8,128)S(1)}, f32[128,512]{1,0:T(8,128)S(1)}, u32[]{:S(2)}, u32[]{:S(2)}) collective-permute-start(f32[128,512]{1,0:T(8,128)S(1)} %get-tuple-element.37.refs_0_), channel_id=1, source_target_pairs={{0,6},{1,7},{2,4},{3,5},{4,2},{5,3},{6,0},{7,1},{8,14},{9,15},{10,... | collective-permute-start | bytes 786440 | tf_op jit(solution)/shard_map/ppermute | solution.py:279
  74.1 17.9 %collective-permute-start.9 = (f32[128,512]{1,0:T(8,128)S(1)}, f32[128,512]{1,0:T(8,128)S(1)}, u32[]{:S(2)}, u32[]{:S(2)}) collective-permute-start(f32[128,512]{1,0:T(8,128)S(1)} %get-tuple-element.37.refs_0_), channel_id=1, source_target_pairs={{0,2},{1,3},{2,0},{3,1},{4,6},{5,7},{6,4},{7,5},{8,10},{9,11},{10,... | collective-permute-start | bytes 786440 | tf_op jit(solution)/shard_map/ppermute | solution.py:279
  75.0 17.0 %collective-permute-start.8 = (f32[256,256]{1,0:T(8,128)S(1)}, f32[256,256]{1,0:T(8,128)S(1)}, u32[]{:S(2)}, u32[]{:S(2)}) collective-permute-start(f32[256,256]{1,0:T(8,128)S(1)} %get-tuple-element.36), channel_id=1, source_target_pairs={{0,8},{1,9},{2,10},{3,11},{4,12},{5,13},{6,14},{7,15},{8,0},{9,1},... | collective-permute-start | bytes 786440 | tf_op jit(solution)/shard_map/ppermute | solution.py:279
  92.4 2.7 %collective-permute-start.12 = (f32[512,512]{1,0:T(8,128)S(1)}, f32[512,512]{1,0:T(8,128)S(1)}, u32[]{:S(2)}, u32[]{:S(2)}) collective-permute-start(f32[512,512]{1,0:T(8,128)S(1)} %shard_map.93), channel_id=1, source_target_pairs={{0,1},{1,0},{2,3},{3,2},{4,5},{5,4},{6,7},{7,6},{8,9},{9,8},{10,11... | collective-permute-start | bytes 3145736 | tf_op jit(solution)/shard_map/ppermute | solution.py:279
  95.6 26.2 %collective-permute-start.13 = (f32[256,512]{1,0:T(8,128)S(1)}, f32[256,512]{1,0:T(8,128)S(1)}, u32[]{:S(2)}, u32[]{:S(2)}) collective-permute-start(f32[256,512]{1,0:T(8,128)S(1)} %get-tuple-element.39), channel_id=1, source_target_pairs={{0,8},{1,9},{2,10},{3,11},{4,12},{5,13},{6,14},{7,15},{8,0},{9,1},... | collective-permute-start | bytes 1572872 | tf_op jit(solution)/shard_map/ppermute | solution.py:279
